TPU v7x, 32 devices: a whole 2x2x4 slice. The times are simulated.
32 devices in a mesh: energy: 4 (over z), cols: 8 (over y, x, core).
Axes of the slice: x: 2, y: 2, z: 4, core: 2. Of those that a mesh axis runs over, the one named last changes fastest.
Arguments:
- left_inverse: bfloat16 [12, 2, 1536, 1536], P('energy', None, 'cols'), parts along dimension 0, as said below
- regions: int32 [3, 1536], replicated, may hold values from 0 to 2
- region_mass: float32 [3], replicated, may hold values from 1 to 2.5
- region_alpha: float32 [3], replicated, may hold values from 0.1 to 0.5
- energy_grid: float32 [16], replicated, may hold values from 0.2 to 1
- energy_index: int32 [4], P('energy'), parts along dimension 0, may hold values from 0 to 15
Outputs:
- green: float32 [8, 2, 1536, 1536], P('energy', None, 'cols'), parts along dimension 0
There are 4 independent parts, one for each index of `energy`. A program takes and returns all parts, laid end to end along the dimension named above; an argument that names none is the same for every part. Nothing has to cross between parts.
Inputs may be any that keep to these rules, and one draw needn't show every extreme that they name: Every block of left_inverse is complex symmetric: both planes equal their transposes.
All inputs are finite; a program needn't handle non-finite values.
Results may differ from a plain program's by a relative error of at most 0.0024.
Values may be sent and summed in bfloat16 or wider, within the bound.
No kernel may reach another device: no remote copies, remote signals or barrier semaphores. Data moves between devices by JAX's collectives and lax.ppermute only.
A program may use at most 128 MiB of HBM per device.

v0:
```python
import jax
import jax.numpy as jnp
from jax import lax
from jax.sharding import PartitionSpec as P


def complex_product(left, right):
    real = jnp.dot(left[0], right[0], preferred_element_type=jnp.float32) - jnp.dot(
        left[1], right[1], preferred_element_type=jnp.float32
    )
    imag = jnp.dot(left[0], right[1], preferred_element_type=jnp.float32) + jnp.dot(
        left[1], right[0], preferred_element_type=jnp.float32
    )
    return jnp.stack([real, imag])


def couplings(regions, region_mass, region_alpha, energy_grid, energy_index):
    level = jnp.sum(
        jnp.where(jnp.arange(energy_grid.shape[0]) == energy_index[0], energy_grid, 0.0)
    )
    onehot = (regions[:, :, None] == jnp.arange(region_mass.shape[0])[None, None, :]).astype(
        jnp.float32
    )
    per_region = region_mass * (1.0 + region_alpha * level)
    mass = jnp.sum(onehot * per_region[None, None, :], axis=2)
    return 2.0 / (mass[:-1] + mass[1:])


def on_device(left_inverse, regions, region_mass, region_alpha, energy_grid, energy_index):
    hop = couplings(regions, region_mass, region_alpha, energy_grid, energy_index)
    count = left_inverse.shape[0]
    own_rows = left_inverse.shape[2]
    offset = lax.axis_index("cols") * own_rows
    own_hop = lax.dynamic_slice_in_dim(hop, offset, own_rows, 1)
    scaled_all = (own_hop[:, None, :, None] * left_inverse[: count - 1].astype(jnp.float32)).astype(
        jnp.bfloat16
    )
    next_green = left_inverse[count - 1]
    blocks = []
    for index in range(count - 2, -1, -1):
        panel = left_inverse[index]
        factor = own_hop[index][None, :, None]
        columns = next_green
        product = complex_product(
            columns, lax.all_gather(scaled_all[index], "cols", axis=1, tiled=True)
        )
        image = (factor * product).astype(jnp.bfloat16)
        coupled = complex_product(panel, lax.all_gather(image, "cols", axis=1, tiled=True))
        current = panel.astype(jnp.float32) + coupled
        blocks.append(current)
        next_green = current.astype(jnp.bfloat16)
    return jnp.stack(blocks[::-1])


def solution(mesh):
    in_specs = (P("energy", None, "cols", None), P(), P(), P(), P(), P("energy"))
    out_specs = P("energy", None, "cols", None)
    return jax.shard_map(
        on_device, mesh=mesh, in_specs=in_specs, out_specs=out_specs, check_vma=False
    )
```

profile of v0, /device:TPU:0, one launch (start us, length us, event | category | flops | bytes accessed | tf_op | source)
XLA Modules:
  0.0 297.7 jit_solution(947890358962893513)
XLA Ops:
  7.2 1.3 fusion.59
  8.5 1.2 add_multiply_fusion
  9.7 0.9 select_reduce_fusion
  10.7 2.2 multiply_convert_fusion
  12.9 1.6 fusion.60
  14.6 61.6 %all-gather.11.cloned.1.call-done = bf16[1,2,1536,1536]{3,2,1,0:T(8,128)(2,1)} async-done(((bf16[1,2,192,1536]{3,2,1,0:T(8,128)(2,1)}), bf16[1,2,1536,1536]{3,2,1,0:T(8,128)(2,1)}) %all-gather.11.cloned.1.call-update) | async-done | bytes 9437200 | tf_op jit(solution)/shard_map/all_gather | solution.py:45
  76.2 3.6 %fusion = f32[1536,192]{0,1:T(8,128)S(1)} fusion(bf16[1,2,1536,1536]{3,2,1,0:T(8,128)(2,1)} %all-gather.11.cloned.1.call-done, bf16[3,2,192,1536]{3,2,1,0:T(8,128)(2,1)S(1)} %copy-done), kind=kOutput, calls=%fused_computation.10 | convolution fusion | flops 905969664 | bytes 6488064 | tf_op jit(solution)/shard_map/dot_general | solution.py:8
  79.8 3.9 %fusion.1 = f32[1536,192]{0,1:T(8,128)S(1)} fusion(bf16[1,2,1536,1536]{3,2,1,0:T(8,128)(2,1)} %all-gather.11.cloned.1.call-done, bf16[3,2,192,1536]{3,2,1,0:T(8,128)(2,1)S(1)} %copy-done), kind=kOutput, calls=%fused_computation.11 | convolution fusion | flops 905969664 | bytes 6488064 | tf_op jit(solution)/shard_map/dot_general | solution.py:11
  83.7 1.1 fusion.24
  84.8 1.1 fusion.25
  86.0 1.3 fusion.32
  87.4 0.7 all-gather.13.cloned.1.call-update
  88.3 58.0 %all-gather.7.cloned.1.call-done = bf16[2,1536,1536]{2,1,0:T(8,128)(2,1)} async-done(((bf16[2,192,1536]{2,1,0:T(8,128)(2,1)}), bf16[2,1536,1536]{2,1,0:T(8,128)(2,1)}) %all-gather.7.cloned.1.call-update) | async-done | bytes 9437200 | tf_op jit(solution)/shard_map/all_gather | solution.py:48
  146.3 3.6 %fusion.4 = f32[1536,192]{0,1:T(8,128)S(1)} fusion(bf16[2,1536,1536]{2,1,0:T(8,128)(2,1)} %all-gather.7.cloned.1.call-done, bf16[3,2,192,1536]{3,2,1,0:T(8,128)(2,1)S(1)} %copy-done), kind=kOutput, calls=%fused_computation.14 | convolution fusion | flops 905969664 | bytes 6488064 | tf_op jit(solution)/shard_map/dot_general | solution.py:8
  149.9 3.9 %fusion.5 = f32[1536,192]{0,1:T(8,128)S(1)} fusion(bf16[2,1536,1536]{2,1,0:T(8,128)(2,1)} %all-gather.7.cloned.1.call-done, bf16[3,2,192,1536]{3,2,1,0:T(8,128)(2,1)S(1)} %copy-done), kind=kOutput, calls=%fused_computation.15 | convolution fusion | flops 905969664 | bytes 6488064 | tf_op jit(solution)/shard_map/dot_general | solution.py:11
  153.8 1.1 fusion.21
  155.0 1.1 fusion.20
  156.1 1.0 copy-done.3
  157.2 1.4 fusion.31
  158.6 48.5 %all-gather.13.cloned.1.call-done = bf16[1,2,1536,1536]{3,2,1,0:T(8,128)(2,1)} async-done(((bf16[1,2,192,1536]{3,2,1,0:T(8,128)(2,1)}), bf16[1,2,1536,1536]{3,2,1,0:T(8,128)(2,1)}) %all-gather.13.cloned.1.call-update) | async-done | bytes 9437200 | tf_op jit(solution)/shard_map/all_gather | solution.py:45
  207.1 3.7 %fusion.9 = f32[192,1536]{1,0:T(8,128)S(1)} fusion(bf16[1,2,1536,1536]{3,2,1,0:T(8,128)(2,1)} %all-gather.13.cloned.1.call-done, bf16[2,192,1536]{2,1,0:T(8,128)(2,1)} %fusion.31), kind=kOutput, calls=%fused_computation.19 | convolution fusion | flops 905969664 | bytes 6488064 | tf_op jit(solution)/shard_map/dot_general | solution.py:8
  210.9 4.2 %fusion.8 = f32[192,1536]{1,0:T(8,128)S(1)} fusion(bf16[1,2,1536,1536]{3,2,1,0:T(8,128)(2,1)} %all-gather.13.cloned.1.call-done, bf16[2,192,1536]{2,1,0:T(8,128)(2,1)S(1)} %copy-done.5), kind=kOutput, calls=%fused_computation.18 | convolution fusion | flops 905969664 | bytes 6488064 | tf_op jit(solution)/shard_map/dot_general | solution.py:11
  215.1 1.1 fusion.27
  216.2 1.1 fusion.26
  217.3 1.3 fusion.33
  218.6 59.0 %all-gather.9.cloned.1.call-done = bf16[2,1536,1536]{2,1,0:T(8,128)(2,1)} async-done(((bf16[2,192,1536]{2,1,0:T(8,128)(2,1)}), bf16[2,1536,1536]{2,1,0:T(8,128)(2,1)}) %all-gather.9.cloned.1.call-update) | async-done | bytes 9437200 | tf_op jit(solution)/shard_map/all_gather | solution.py:48
  277.6 3.6 %fusion.12 = f32[1536,192]{0,1:T(8,128)S(1)} fusion(bf16[2,1536,1536]{2,1,0:T(8,128)(2,1)} %all-gather.9.cloned.1.call-done, bf16[3,2,192,1536]{3,2,1,0:T(8,128)(2,1)S(1)} %copy-done), kind=kOutput, calls=%fused_computation.22 | convolution fusion | flops 905969664 | bytes 6488064 | tf_op jit(solution)/shard_map/dot_general | solution.py:8
  281.2 3.9 %fusion.13 = f32[1536,192]{0,1:T(8,128)S(1)} fusion(bf16[2,1536,1536]{2,1,0:T(8,128)(2,1)} %all-gather.9.cloned.1.call-done, bf16[3,2,192,1536]{3,2,1,0:T(8,128)(2,1)S(1)} %copy-done), kind=kOutput, calls=%fused_computation.23 | convolution fusion | flops 905969664 | bytes 6488064 | tf_op jit(solution)/shard_map/dot_general | solution.py:11
  285.1 1.1 fusion.28
  286.3 1.1 fusion.29
  287.9 0.8 maximum_add_fusion
  288.7 2.5 pad_maximum_fusion
  (29 shorter events, 1.0 us)
Async XLA Ops:
  6.5 69.7 %all-gather.11.cloned.1.call-start = ((), (), s32[]{:S(2)}) async-start(), calls=%async_computation.2 | async-start | bytes 10616832 | tf_op jit(solution)/shard_map/all_gather | solution.py:45
  12.9 63.3 %copy-start = (bf16[3,2,192,1536]{3,2,1,0:T(8,128)(2,1)S(1)}, bf16[3,2,192,1536]{3,2,1,0:T(8,128)(2,1)}, u32[]{:S(2)}) copy-start(bf16[3,2,192,1536]{3,2,1,0:T(8,128)(2,1)} %param.6) | copy-start | bytes 10616836
  14.5 131.8 %all-gather.7.cloned.1.call-start = ((), (), s32[]{:S(2)}) async-start(), calls=%async_computation | async-start | bytes 10616832 | tf_op jit(solution)/shard_map/all_gather | solution.py:48
  76.2 7.5 %copy-start.8 = (bf16[1,2,1536,1536]{3,2,1,0:T(8,128)(2,1)S(1)}, bf16[1,2,1536,1536]{3,2,1,0:T(8,128)(2,1)}, u32[]{:S(2)}) copy-start(bf16[1,2,1536,1536]{3,2,1,0:T(8,128)(2,1)} %all-gather.11.cloned.1.call-done) | copy-start | bytes 28311556
  87.3 119.8 %all-gather.13.cloned.1.call-start = ((), (), s32[]{:S(2)}) async-start(), calls=%async_computation.3 | async-start | bytes 10616832 | tf_op jit(solution)/shard_map/all_gather | solution.py:45
  88.1 189.5 %all-gather.9.cloned.1.call-start = ((), (), s32[]{:S(2)}) async-start(), calls=%async_computation.1 | async-start | bytes 10616832 | tf_op jit(solution)/shard_map/all_gather | solution.py:48
  146.3 7.5 %copy-start.7 = (bf16[2,1536,1536]{2,1,0:T(8,128)(2,1)S(1)}, bf16[2,1536,1536]{2,1,0:T(8,128)(2,1)}, u32[]{:S(2)}) copy-start(bf16[2,1536,1536]{2,1,0:T(8,128)(2,1)} %all-gather.7.cloned.1.call-done) | copy-start | bytes 28311556
  155.0 1.1 copy-start.1
  156.1 1.1 copy-start.3
  207.1 3.8 %copy-start.5 = (bf16[2,192,1536]{2,1,0:T(8,128)(2,1)S(1)}, bf16[2,192,1536]{2,1,0:T(8,128)(2,1)}, u32[]{:S(2)}) copy-start(bf16[2,192,1536]{2,1,0:T(8,128)(2,1)} %fusion.31) | copy-start | bytes 3538948
  207.1 7.9 %copy-start.6 = (bf16[1,2,1536,1536]{3,2,1,0:T(8,128)(2,1)S(1)}, bf16[1,2,1536,1536]{3,2,1,0:T(8,128)(2,1)}, u32[]{:S(2)}) copy-start(bf16[1,2,1536,1536]{3,2,1,0:T(8,128)(2,1)} %all-gather.13.cloned.1.call-done) | copy-start | bytes 28311556
  277.6 7.5 %copy-start.9 = (bf16[2,1536,1536]{2,1,0:T(8,128)(2,1)S(1)}, bf16[2,1536,1536]{2,1,0:T(8,128)(2,1)}, u32[]{:S(2)}) copy-start(bf16[2,1536,1536]{2,1,0:T(8,128)(2,1)} %all-gather.9.cloned.1.call-done) | copy-start | bytes 28311556
  286.2 1.3 copy-start.2
  286.3 1.6 copy-start.4
Sparse Core Ops, SparseCore 0:
  14.6 61.5 all-gather.10
  87.5 58.8 all-gather.6
  148.2 58.8 all-gather.12
  218.7 58.8 all-gather.8
where the time goes:
time: 298 us
  waiting for transfers between devices  228 us (77%)
  matrix products  39.3 us (13%)
  between operations  14 us (5%)
  other arithmetic  13.1 us (4%)
  local copies, waits for them, and re-layouts  3.17 us (1%)
    all_gather x2, waiting for transfers between devices, on_device(): lax.all_gather(image, 'cols', axis=1, tiled=True)  117 us
    all_gather x2, waiting for transfers between devices, on_device(): lax.all_gather(scaled_all[index], 'cols', axis=1, tiled=True)  110 us
    dot_general x4, matrix products, complex_product(): jnp.dot(left[1], right[0], preferred_element_type=jnp.float32)  16 us
    dot_general x4, matrix products, complex_product(): jnp.dot(left[0], right[0], preferred_element_type=jnp.float32)  14.4 us
  transfers between devices with their start and end apart: 4, of which 4 were waited for; matrix products, arithmetic and copies ran while one was open for 4% of the time, Pallas kernels for 0%

commit v1 on v0

v1 whole, which is shorter than its diff:
```python
import functools

import jax
import jax.numpy as jnp
from jax import lax
from jax.experimental import pallas as pl
from jax.experimental.pallas import tpu as pltpu
from jax.sharding import PartitionSpec as P

F32 = jnp.float32
BF16 = jnp.bfloat16
F8 = jnp.float8_e5m2
F8_MAX = 57344.0
LOW = 512.0
DIAG = 16
ORDER = (1, 2, 0)
PAD = 16
VMEM = pl.BlockSpec(memory_space=pltpu.VMEM)
SMEM = pl.BlockSpec(memory_space=pltpu.SMEM)
ANY = pl.BlockSpec(memory_space=pl.ANY)
HBM = pl.BlockSpec(memory_space=pltpu.HBM)


def params(mib=56):
    return pltpu.CompilerParams(vmem_limit_bytes=mib * 2**20)


def cost(flops, moved):
    return pl.CostEstimate(flops=flops, bytes_accessed=moved, transcendentals=0)


def couplings(regions, region_mass, region_alpha, energy_grid, energy_index):
    level = jnp.sum(
        jnp.where(jnp.arange(energy_grid.shape[0]) == energy_index[0], energy_grid, 0.0)
    )
    onehot = (regions[:, :, None] == jnp.arange(region_mass.shape[0])[None, None, :]).astype(F32)
    per_region = region_mass * (1.0 + region_alpha * level)
    mass = jnp.sum(onehot * per_region[None, None, :], axis=2)
    return 2.0 / (mass[:-1] + mass[1:])


def product(left, right):
    real = jnp.dot(left[0], right[0], preferred_element_type=F32) - jnp.dot(
        left[1], right[1], preferred_element_type=F32
    )
    imag = jnp.dot(left[0], right[1], preferred_element_type=F32) + jnp.dot(
        left[1], right[0], preferred_element_type=F32
    )
    return jnp.stack([real, imag])


def general(left_inverse, regions, region_mass, region_alpha, energy_grid, energy_index):
    hop = couplings(regions, region_mass, region_alpha, energy_grid, energy_index)
    count = left_inverse.shape[0]
    whole = [None] * count
    for index in list(range(count - 2, -1, -1)) + [count - 1]:
        whole[index] = lax.all_gather(left_inverse[index], "cols", axis=1, tiled=True)
    blocks = []
    for index in range(count - 2, -1, -1):
        rows = left_inverse[index].astype(F32)

        def times_green(left, level):
            if level == count - 1:
                return product(left, whole[level])
            first = product(left, whole[level])
            inner = times_green((first * hop[level]).astype(BF16), level + 1)
            return first + product((inner * hop[level]).astype(BF16), whole[level])

        inner = times_green((rows * hop[index]).astype(BF16), index + 1)
        blocks.append(rows + product((inner * hop[index]).astype(BF16), whole[index]))
    return jnp.stack(blocks[::-1])


TILE = 512
LIMITS = (16, 16, 22, 24, 20)


class Sizes:
    def __init__(self, rows, size):
        self.rows = rows
        self.chip = 2 * rows
        self.size = size
        self.head = rows + DIAG
        self.slab = rows * 4 + DIAG


def own_part(idx_ref):
    index = idx_ref[0]
    return lax.div(index, 2), lax.rem(index, 2)


def columns(chip, other, s):
    return pl.ds(pl.multiple_of(jnp.bitwise_xor(chip, other) * s.chip, 128), s.chip)


class Copies:
    def __init__(self, sems):
        self.sems = sems
        self.made = []

    def start(self, source, target):
        copy = pltpu.make_async_copy(source, target, self.sems.at[len(self.made)])
        copy.start()
        self.made.append([copy, False])
        return len(self.made) - 1

    def wait(self, which=None):
        for i in range(len(self.made)) if which is None else which:
            copy, done = self.made[i]
            if not done:
                copy.wait()
                self.made[i][1] = True


def pack_kernel(s, index, heads, idx_ref, a_ref, *refs):
    n = 3 if heads else 2
    outs, buffers, (planes, sems) = refs[:n], refs[n : 2 * n], refs[2 * n :]
    xs, ys = buffers[:2]
    chip, core = own_part(idx_ref)
    r = s.rows
    copies = Copies(sems)
    blocks = heads or (index,)
    loads = [
        copies.start(a_ref.at[block, :, :, columns(chip, 0, s)], planes.at[i])
        for i, block in enumerate(blocks)
    ]
    for plane in (0, 1):
        here = pl.ds(s.head + plane * r, r)
        copies.start(a_ref.at[index, plane, :, columns(chip, 2, s)], xs.at[here, :])
        copies.start(a_ref.at[index, plane, :, columns(chip, 1, s)], ys.at[here, :])
    here = pl.ds(s.head + 2 * r, r)
    copies.start(a_ref.at[index, 0, :, columns(chip, 3, s)], xs.at[here, :])
    copies.start(a_ref.at[index, 1, :, columns(chip, 3, s)], ys.at[here, :])
    row = lax.broadcasted_iota(jnp.int32, (r, s.chip), 0) + core * r
    col = lax.broadcasted_iota(jnp.int32, (r, s.chip), 1)
    for i, block in enumerate(blocks):
        copies.wait([loads[i]])
        real = planes[i, 0].astype(F32)
        imag = planes[i, 1].astype(F32)
        head = jnp.where(col >= row, real, imag).astype(BF16)
        diag = jnp.sum(jnp.where(col == row, imag, 0.0), axis=0, keepdims=True)
        diag = jnp.broadcast_to(diag, (DIAG, s.chip)).astype(BF16)
        places = [(xs, 0), (ys, 0)] if block == index else []
        if heads:
            places.append((buffers[2], i * s.head))
        for buffer, start in places:
            buffer[start : start + r, :] = head
            buffer[start + r : start + s.head, :] = diag
    for buffer in (xs, ys):
        if buffer.shape[0] > s.slab:
            buffer[s.slab :, :] = jnp.zeros((buffer.shape[0] - s.slab, s.chip), BF16)
    copies.wait()
    for buffer, out in zip(buffers, outs):
        copies.start(buffer, out)
    copies.wait()


def pack(s, idx, a, index, heads):
    rows = s.slab + PAD * ORDER.index(index)
    shapes = [jax.ShapeDtypeStruct((k, s.chip), BF16) for k in (rows, rows, len(heads) * s.head)]
    if not heads:
        shapes.pop()
    return list(
        pl.pallas_call(
            functools.partial(pack_kernel, s, index, heads),
            in_specs=[SMEM, HBM],
            out_specs=[ANY] * len(shapes),
            out_shape=shapes,
            scratch_shapes=[pltpu.VMEM(x.shape, BF16) for x in shapes]
            + [
                pltpu.VMEM((max(1, len(heads)), 2, s.rows, s.chip), BF16),
                pltpu.SemaphoreType.DMA((12,)),
            ],
            compiler_params=params(LIMITS[0]),
            cost_estimate=cost(0, 0),
            name="pack",
        )(idx, a)
    )


def gate_kernel(*refs):
    pass


def gate(buffers, tokens):
    n = len(buffers)
    return list(pl.pallas_call(
        gate_kernel,
        in_specs=[ANY] * (n + len(tokens)),
        out_specs=[ANY] * n,
        out_shape=[jax.ShapeDtypeStruct(b.shape, b.dtype) for b in buffers],
        input_output_aliases={i: i for i in range(n)},
        compiler_params=params(1),
        cost_estimate=cost(0, 0),
        name="gate",
    )(*buffers, *tokens))


def put_split(hi_ref, lo_ref, rows, cols, value):
    hi = value.astype(BF16)
    hi_ref[rows, cols] = hi
    if lo_ref is None:
        return
    rest = (value - hi.astype(F32)) * LOW
    lo_ref[rows, cols] = jnp.clip(rest, -F8_MAX, F8_MAX).astype(F8)


def prep_kernel(
    s, idx_ref, index_ref, grid_ref, mass_ref, alpha_ref, regions_ref, a_ref, _, hop_out, down_out, s0_hi, s0_lo, s1_ref
):
    chip, _ = own_part(idx_ref)
    r = s.rows
    level = grid_ref[index_ref[0]]
    for other in range(4):
        cols = columns(chip, other, s)
        regions = regions_ref[:, cols]
        mass = jnp.zeros(regions.shape, F32)
        for region in range(mass_ref.shape[0]):
            value = mass_ref[region] * (1.0 + alpha_ref[region] * level)
            mass = jnp.where(regions == region, value, mass)
        hop = 2.0 / (mass[:-1] + mass[1:])
        here = slice(other * s.chip, (other + 1) * s.chip)
        hop_out[:, here] = hop
        for index in (0, 1):
            down_out[index, here, :] = jnp.broadcast_to(hop[index : index + 1, :], (128, s.chip)).T
            for plane in (0, 1):
                part = a_ref[index, plane, :, cols].astype(F32) * hop[index : index + 1, :]
                rows = slice(plane * r, (plane + 1) * r)
                hi, lo = ((s0_hi, s0_lo), (s1_ref, None))[index]
                put_split(hi, lo, rows, here, part)


def full(x):
    return pl.BlockSpec(x.shape, lambda i: (0,) * x.ndim)


def prep(s, idx, a, regions, region_mass, region_alpha, energy_grid, energy_index, token):
    shapes = [
        jax.ShapeDtypeStruct((regions.shape[0] - 1, regions.shape[1]), F32),
        jax.ShapeDtypeStruct((regions.shape[0] - 1, regions.shape[1], 128), F32),
    ] + split_shapes(s) + split_shapes(s)[:1]
    return pl.pallas_call(
        functools.partial(prep_kernel, s),
        grid=(1,),
        in_specs=[SMEM] * 5
        + [full(regions), pl.BlockSpec((2,) + a.shape[1:], lambda i: (0, 0, 0, 0)), ANY],
        out_specs=[full(x) for x in shapes],
        out_shape=shapes,
        compiler_params=params(16),
        cost_estimate=cost(0, 0),
        name="prep",
    )(idx, energy_index, energy_grid, region_mass, region_alpha, regions, a, token)


def split_shapes(s):
    return [jax.ShapeDtypeStruct((s.chip, s.size), kind) for kind in (BF16, F8)]


PIECES = 40


def start_pieces(s, chip, core, index, rows_refs, sides, z_at, whole, diags, copies):
    r, m = s.rows, s.chip

    def cols(other):
        return pl.ds(other * m, m)

    for side, (offset, ref, (xs, ys, z)) in enumerate(
        zip((core * r, (1 - core) * r), rows_refs, sides)
    ):

        def rows(base):
            return pl.ds(pl.multiple_of(base + offset, 16), r)

        for other in range(4):
            copies.start(
                ref.at[index, :, :, columns(chip, other, s)], whole.at[:, rows(0), cols(other)]
            )
        for which, got, at in ((1, xs, 0), (2, ys, 0), (3, z, z_at)):
            copies.start(got.at[pl.ds(at, r), :], whole.at[0, rows(which * m), cols(which)])
            copies.start(got.at[pl.ds(at + r, DIAG), :], diags.at[which - 1, side])
            if which == 3:
                continue
            for plane in (0, 1):
                copies.start(
                    got.at[pl.ds(s.head + plane * r, r), :],
                    whole.at[plane, rows(which * m), cols(3)],
                )
            copies.start(
                got.at[pl.ds(s.head + 2 * r, r), :],
                whole.at[which - 1, rows(which * m), cols(3 - which)],
            )


def complete(s, whole, diags):
    m = s.chip
    row = lax.broadcasted_iota(jnp.int32, (m, m), 0)
    col = lax.broadcasted_iota(jnp.int32, (m, m), 1)
    for which in (1, 2, 3):
        here = slice(which * m, (which + 1) * m)
        packed = whole[0, here, here].astype(F32)
        flipped = packed.T
        diag = diags[which - 1, 0].astype(F32) + diags[which - 1, 1].astype(F32)
        diag = jnp.broadcast_to(diag[0:1, :], (m, m))
        real = jnp.where(col >= row, packed, flipped)
        imag = jnp.where(col < row, packed, jnp.where(col > row, flipped, diag))
        whole[0, here, here] = real.astype(BF16)
        whole[1, here, here] = imag.astype(BF16)
    for plane in (0, 1):
        for a, b in ((0, 1), (0, 2), (0, 3), (1, 3), (2, 3), (1, 2) if plane == 0 else (2, 1)):
            block = whole[plane, a * m : (a + 1) * m, b * m : (b + 1) * m]
            whole[plane, b * m : (b + 1) * m, a * m : (a + 1) * m] = block.T


def multiply(lefts, right, s):
    r = s.rows
    if any(lo is not None for _, lo in lefts):
        small = [jnp.clip(plane, -F8_MAX, F8_MAX).astype(F8) for plane in right]
    out = []
    for hi, lo in lefts:
        by = [jnp.dot(hi[...], plane, preferred_element_type=F32) for plane in right]
        if lo is not None:
            by = [
                part + jnp.dot(lo[...], low, preferred_element_type=F32) * (1.0 / LOW)
                for part, low in zip(by, small)
            ]
        out.append((by[0][:r] - by[1][r:], by[1][:r] + by[0][r:]))
    return out


def planes(whole, cols):
    return [whole[plane, :, cols] for plane in (0, 1)]


def segments(start, width, s):
    at, out = start, []
    while at < start + width:
        other = at // s.chip
        stop = min(start + width, (other + 1) * s.chip)
        out.append((at, stop - at, other, at - other * s.chip))
        at = stop
    return out


def first_kernel(s, idx_ref, hop_ref, down_ref, hi, lo, *refs):
    own, own_c, x1, x1_c, y1, y1_c, z, z_c = refs[:8]
    scaled, x, w_hi, w_lo, whole, diags, sems = refs[8:]
    chip, core = own_part(idx_ref)
    r, n = s.rows, s.size
    copies = Copies(sems)
    sides = ((x1, y1, z), (x1_c, y1_c, z_c))
    start_pieces(s, chip, core, 1, (own, own_c), sides, 0, whole, diags, copies)
    copies.wait()
    complete(s, whole, diags)
    for t in range(0, n, TILE):
        cols = slice(t, t + TILE)
        right = planes(whole, cols)
        (parts,) = multiply([(hi, lo)], right, s)
        for plane, part in enumerate(parts):
            here = slice(plane * r, (plane + 1) * r)
            x[here, cols] = part
            put_split(w_hi, w_lo, here, cols, part * hop_ref[1:2, cols])
            scaled[plane, :, cols] = scale_rows(right[plane], down_ref, 1)


def scale_rows(plane, down_ref, index):
    return (plane.astype(F32) * down_ref[index, :, 0:1]).astype(BF16)


def second_kernel(s, idx_ref, s1_ref, w_hi, w_lo, *refs):
    own, own_c, x2, x2_c, y2, y2_c, z, z_c = refs[:8]
    u_ref, y_hi, y_lo, whole, diags, sems = refs[8:]
    chip, core = own_part(idx_ref)
    r, n = s.rows, s.size
    copies = Copies(sems)
    sides = ((x2, y2, z), (x2_c, y2_c, z_c))
    start_pieces(s, chip, core, 2, (own, own_c), sides, s.head, whole, diags, copies)
    copies.wait()
    complete(s, whole, diags)
    for t in range(0, n, TILE):
        cols = slice(t, t + TILE)
        u, y = multiply([(s1_ref, None), (w_hi, w_lo)], planes(whole, cols), s)
        for plane in (0, 1):
            here = slice(plane * r, (plane + 1) * r)
            put_split(u_ref, None, here, cols, u[plane])
            put_split(y_hi, y_lo, here, cols, y[plane])


def third_kernel(s, hi, lo, scaled, x, v_hi, v_lo):
    r, n = s.rows, s.size
    for t in range(0, n, TILE):
        cols = slice(t, t + TILE)
        (parts,) = multiply([(hi, lo)], planes(scaled, cols), s)
        for plane in (0, 1):
            here = slice(plane * r, (plane + 1) * r)
            put_split(v_hi, v_lo, here, cols, x[here, cols] + parts[plane])


def start_own(s, chip, a_ref, index, own, copies):
    return [
        copies.start(
            a_ref.at[index, :, :, columns(chip, other, s)],
            own.at[:, :, pl.ds(other * s.chip, s.chip)],
        )
        for other in range(4)
    ]


def green_kernel(s, idx_ref, left, scaled, a_ref, g1, own, sems):
    chip, core = own_part(idx_ref)
    copies = Copies(sems)
    mine = start_own(s, chip, a_ref, 1, own, copies)
    for t in range(0, s.size, TILE):
        (parts,) = multiply([(left, None)], planes(scaled, slice(t, t + TILE)), s)
        copies.wait(mine)
        add_own(s, own, parts, t, TILE, g1)


def add_own(s, own, parts, start, width, g_ref):
    cols = slice(start, start + width)
    for plane in (0, 1):
        g_ref[plane, :, cols] = own[plane, :, cols].astype(F32) + parts[plane]


def send_out(s, chip, start, width, g_ref, out_ref, index, copies):
    for at, size, other, offset in segments(start, width, s):
        base = jnp.bitwise_xor(chip, other) * s.chip + offset
        where = pl.ds(pl.multiple_of(base, 128), size)
        copies.start(g_ref.at[:, :, pl.ds(at, size)], out_ref.at[index, :, :, where])


def last_kernel(s, idx_ref, down_ref, hi, lo, g1, *refs):
    rows, rows_c, x0, x0_c, y0, y0_c, z, z_c = refs[:8]
    out_ref, whole, diags, own, g0, sems = refs[8:]
    chip, core = own_part(idx_ref)
    copies = Copies(sems)
    sides = ((x0, y0, z), (x0_c, y0_c, z_c))
    start_pieces(s, chip, core, 0, (rows, rows_c), sides, 0, whole, diags, copies)
    start_own(s, chip, rows, 0, own, copies)
    copies.wait()
    send_out(s, chip, 0, s.size, g1, out_ref, 1, copies)
    complete(s, whole, diags)
    width = TILE // 2
    for t in range(0, s.size, width):
        cols = slice(t, t + width)
        right = [scale_rows(plane, down_ref, 0) for plane in planes(whole, cols)]
        (parts,) = multiply([(hi, lo)], right, s)
        add_own(s, own, parts, t, width, g0)
        send_out(s, chip, t, width, g0, out_ref, 0, copies)
    copies.wait()


def swap(x, mask, n=8):
    return lax.ppermute(x, "cols", [(i, i ^ mask) for i in range(n)])


def special(left_inverse, regions, region_mass, region_alpha, energy_grid, energy_index):
    a = left_inverse
    s = Sizes(a.shape[2], a.shape[3])
    idx = lax.axis_index("cols").astype(jnp.int32)[None]
    n, m, r = s.size, s.chip, s.rows

    a_cross = swap(a, 1)
    x1, y1, z = pack(s, idx, a, 1, (1, 2))
    x1, y1, z = swap(x1, 2), swap(y1, 4), swap(z, 6)
    x2, y2 = pack(s, idx, a, 2, ())
    x0, y0, z0 = pack(s, idx, a, 0, (0,))
    hop, down, s0_hi, s0_lo, s1 = prep(
        s, idx, a, regions, region_mass, region_alpha, energy_grid, energy_index, a_cross
    )
    x1, y1, z = gate([x1, y1, z], (hop, x0, x2))
    x2, y2 = swap(x2, 2), swap(y2, 4)
    z_cross = swap(z, 1)

    split = split_shapes(s)
    block = jax.ShapeDtypeStruct((2, n, n), BF16)
    whole = pltpu.VMEM(block.shape, BF16)
    diags = pltpu.VMEM((3, 2, DIAG, m), BF16)
    own = pltpu.VMEM((2, r, n), BF16)
    sems = pltpu.SemaphoreType.DMA((PIECES + 20,))

    def call(kernel, name, ins, pieces, out_specs, out_shape, scratch, limit):
        return pl.pallas_call(
            functools.partial(kernel, s),
            in_specs=[SMEM if x is idx else HBM if x is a else VMEM for x in ins]
            + [HBM if x is a or x is a_cross else ANY for x in pieces],
            out_specs=out_specs,
            out_shape=out_shape,
            scratch_shapes=scratch,
            compiler_params=params(limit),
            cost_estimate=cost(0, 0),
            name=name,
        )(*ins, *pieces)

    scaled, x, w_hi, w_lo = call(
        first_kernel,
        "first",
        [idx, hop, down, s0_hi, s0_lo],
        [a, a_cross, x1, swap(x1, 1), y1, swap(y1, 1), z, z_cross],
        [VMEM] * 4,
        [block, jax.ShapeDtypeStruct((m, n), F32)] + split,
        [whole, diags, sems],
        LIMITS[1],
    )
    x0, y0, z0 = gate([x0, y0, z0], (z_cross,))
    x0, y0, z0 = swap(x0, 2), swap(y0, 4), swap(z0, 6)
    x2, y2 = gate([x2, y2], (w_hi,))
    u, y_hi, y_lo = call(
        second_kernel,
        "second",
        [idx, s1, w_hi, w_lo],
        [a, a_cross, x2, swap(x2, 1), y2, swap(y2, 1), z, z_cross],
        [VMEM] * 3,
        split[:1] + split,
        [whole, diags, sems],
        LIMITS[2],
    )
    v_hi, v_lo = call(
        third_kernel, "third", [y_hi, y_lo, scaled, x], [], [VMEM] * 2, split, [], LIMITS[3]
    )
    x0, y0, z0 = gate([x0, y0, z0], (v_hi,))
    green = jax.ShapeDtypeStruct((2, r, n), F32)
    g1 = call(
        green_kernel, "green_1", [idx, u, scaled, a], [], VMEM, green, [own, sems], LIMITS[3]
    )
    return call(
        last_kernel,
        "green_0",
        [idx, down, v_hi, v_lo, g1],
        [a, a_cross, x0, swap(x0, 1), y0, swap(y0, 1), z0, swap(z0, 1)],
        HBM,
        jax.ShapeDtypeStruct((2, 2, r, n), F32),
        [whole, diags, own, pltpu.VMEM((2, r, n), F32), sems],
        LIMITS[4],
    )


def solution(mesh):
    def on_device(left_inverse, *rest):
        rows = left_inverse.shape[2]
        if mesh.shape["cols"] == 8 and left_inverse.shape[0] == 3 and rows % 64 == 0:
            return special(left_inverse, *rest)
        return general(left_inverse, *rest)

    in_specs = (P("energy", None, "cols", None), P(), P(), P(), P(), P("energy"))
    out_specs = P("energy", None, "cols", None)
    return jax.shard_map(
        on_device, mesh=mesh, in_specs=in_specs, out_specs=out_specs, check_vma=False
    )
```

time: 298 us -> 79.1 us (0.27)
  waiting for transfers between devices: 228 us -> 18 us
  Pallas kernels: 0 us -> 44.3 us
  matrix products: 39.3 us -> 0 us
  other arithmetic: 13.1 us -> 0 us
  starting transfers between devices: 0.3 us -> 13.4 us
  between operations: 14 us -> 1.07 us
    all_gather x4 -> x0, waiting for transfers between devices: 227 us -> none  [the longest x2 117 us: on_device(): lax.all_gather(image, 'cols', axis=1, tiled=True)]
    pallas_call x0 -> x13, Pallas kernels: none -> 44.3 us  [the longest x5 40.3 us: call(): pl.pallas_call(functools.partial(kernel, s), in_specs=[SMEM if x is idx e...]
    dot_general x16 -> x0, matrix products: 39.3 us -> none  [the longest x4 16 us: complex_product(): jnp.dot(left[1], right[0], preferred_element_type=jnp.float32)]
    ppermute x0 -> x17, waiting for transfers between devices: none -> 18 us  [swap(): return lax.ppermute(x, 'cols', [(i, i ^ mask) for i in range(n)])]
    ppermute x0 -> x17, starting transfers between devices: none -> 13.4 us  [swap(): return lax.ppermute(x, 'cols', [(i, i ^ mask) for i in range(n)])]
    convert_element_type x4 -> x0, other arithmetic: 6.31 us -> none  [the longest x2 2.65 us: on_device(): image = (factor * product).astype(jnp.bfloat16)]
  transfers between devices with their start and end apart: 4 -> 17, of which waited for: 4 -> 5; matrix products, arithmetic and copies ran while one was open for 4% -> 0% of each run, Pallas kernels for 0% -> 45%
where the time goes in v1:
time: 79.1 us; the launch traced here: 78.9 us
  Pallas kernels  44.3 us (56%)
  waiting for transfers between devices  18 us (23%)
  starting transfers between devices  13.4 us (17%)
  local copies, waits for them, and re-layouts  2.03 us (3%)
  between operations  1.07 us (1%)
    pallas_call x5, Pallas kernels, call(): pl.pallas_call(functools.partial(kernel, s), in_specs=[SMEM if x is idx e...  40.3 us
    ppermute x17, waiting for transfers between devices, swap(): return lax.ppermute(x, 'cols', [(i, i ^ mask) for i in range(n)])  18 us
    ppermute x17, starting transfers between devices, swap(): return lax.ppermute(x, 'cols', [(i, i ^ mask) for i in range(n)])  13.4 us
    pallas_call x3, Pallas kernels, pack(): pl.pallas_call(functools.partial(pack_kernel, s, index, heads), in_specs=...  2.37 us
    unnamed x12, local copies, waits for them, and re-layouts  2.03 us
    pallas_call x1, Pallas kernels, prep(): pl.pallas_call(functools.partial(prep_kernel, s), grid=(1,), in_specs=[SM...  1.61 us
  transfers between devices with their start and end apart: 17, of which 5 were waited for; matrix products, arithmetic and copies ran while one was open for 0% of the time, Pallas kernels for 45%

profile of v1, /device:TPU:0, one launch (start us, length us, event | category | flops | bytes accessed | tf_op | source)
XLA Modules:
  0.0 78.9 jit_solution(6336894765102241424)
XLA Ops:
  0.0 0.5 collective-permute-start
  0.5 2.0 %copy-done = bf16[3,2,192,1536]{3,2,1,0:T(8,128)(2,1)S(1)} copy-done((bf16[3,2,192,1536]{3,2,1,0:T(8,128)(2,1)S(1)}, bf16[3,2,192,1536]{3,2,1,0:T(8,128)(2,1)}, u32[]{:S(2)}) %copy-start) | copy-done | bytes 3538968
  2.5 0.8 %pack.3 = (bf16[784,384]{1,0:T(8,128)(2,1)S(1)}, bf16[784,384]{1,0:T(8,128)(2,1)S(1)}, bf16[416,384]{1,0:T(8,128)(2,1)S(1)}) custom-call(s32[1]{0:T(128)} %bitcast.idx_ref, bf16[3,2,192,1536]{3,2,1,0:T(8,128)(2,1)S(1)} %copy-done), custom_call_target="tpu_custom_call" | custom-call | tf_op jit(solution)/shard_map/pack/pallas_call | solution.py:164
  3.3 2.6 %collective-permute-start.1 = (bf16[784,384]{1,0:T(8,128)(2,1)S(1)}, bf16[784,384]{1,0:T(8,128)(2,1)S(1)}, u32[]{:S(2)}, u32[]{:S(2)}) collective-permute-start(bf16[784,384]{1,0:T(8,128)(2,1)S(1)} %get-tuple-element.43), channel_id=1, source_target_pairs={{0,2},{1,3},{2,0},{3,1},{4,6},{5,7},{6,4},{7,5},{8,10},{9,11},{10,... | collective-permute-start | bytes 1806344 | tf_op jit(solution)/shard_map/ppermute | solution.py:454
  5.9 1.5 %collective-permute-start.2 = (bf16[784,384]{1,0:T(8,128)(2,1)S(1)}, bf16[784,384]{1,0:T(8,128)(2,1)S(1)}, u32[]{:S(2)}, u32[]{:S(2)}) collective-permute-start(bf16[784,384]{1,0:T(8,128)(2,1)S(1)} %get-tuple-element.44), channel_id=1, source_target_pairs={{0,4},{1,5},{2,6},{3,7},{4,0},{5,1},{6,2},{7,3},{8,12},{9,13},{10,... | collective-permute-start | bytes 1806344 | tf_op jit(solution)/shard_map/ppermute | solution.py:454
  7.4 0.0 collective-permute-start.3
  7.4 0.6 pack.5
  8.1 0.0 copy-start.1
  8.1 0.0 copy-start.3
  8.1 2.0 %collective-permute-start.8 = (bf16[800,384]{1,0:T(8,128)(2,1)S(1)}, bf16[800,384]{1,0:T(8,128)(2,1)S(1)}, u32[]{:S(2)}, u32[]{:S(2)}) collective-permute-start(bf16[800,384]{1,0:T(8,128)(2,1)S(1)} %get-tuple-element.53), channel_id=1, source_target_pairs={{0,4},{1,5},{2,6},{3,7},{4,0},{5,1},{6,2},{7,3},{8,12},{9,13},{10,... | collective-permute-start | bytes 1843208 | tf_op jit(solution)/shard_map/ppermute | solution.py:454
  10.2 0.9 %pack.4 = (bf16[816,384]{1,0:T(8,128)(2,1)S(1)}, bf16[816,384]{1,0:T(8,128)(2,1)S(1)}, bf16[208,384]{1,0:T(8,128)(2,1)S(1)}) custom-call(s32[1]{0:T(128)} %bitcast.idx_ref, bf16[3,2,192,1536]{3,2,1,0:T(8,128)(2,1)S(1)} %copy-done), custom_call_target="tpu_custom_call" | custom-call | tf_op jit(solution)/shard_map/pack/pallas_call | solution.py:164
  11.1 1.6 %collective-permute-start.7 = (bf16[800,384]{1,0:T(8,128)(2,1)S(1)}, bf16[800,384]{1,0:T(8,128)(2,1)S(1)}, u32[]{:S(2)}, u32[]{:S(2)}) collective-permute-start(bf16[800,384]{1,0:T(8,128)(2,1)S(1)} %get-tuple-element.47.refs_5_), channel_id=1, source_target_pairs={{0,2},{1,3},{2,0},{3,1},{4,6},{5,7},{6,4},{7,5},{8,10},{9,11},{10,... | collective-permute-start | bytes 1843208 | tf_op jit(solution)/shard_map/ppermute | solution.py:454
  13.3 1.6 %prep.1 = (f32[2,1536]{1,0:T(2,128)S(1)}, f32[2,1536,128]{2,1,0:T(8,128)S(1)}, bf16[384,1536]{1,0:T(8,128)(2,1)S(1)}, f8e5m2[384,1536]{1,0:T(32,128)(4,1)S(1)}, bf16[384,1536]{1,0:T(8,128)(2,1)S(1)}) custom-call(s32[1]{0:T(128)} %bitcast.idx_ref, s32[1]{0:T(128)S(6)} %copy.29.index_ref, f32[16]{0:T(128)S(1)} %copy-done.3, f32[3]{0:T(128)S(1)} %copy-done.4, ...), custom_call_target="tpu_custom_call" | custom-call | tf_op jit(solution)/shard_map/prep/pallas_call | solution.py:242
  14.9 13.7 %collective-permute-done.3.refs_2_ = bf16[416,384]{1,0:T(8,128)(2,1)S(1)} collective-permute-done((bf16[416,384]{1,0:T(8,128)(2,1)S(1)}, bf16[416,384]{1,0:T(8,128)(2,1)S(1)}, u32[]{:S(2)}, u32[]{:S(2)}) %collective-permute-start.3) | collective-permute-done | bytes 319520 | tf_op jit(solution)/shard_map/ppermute | solution.py:454
  28.6 0.5 collective-permute-done.2.refs_1_
  29.1 0.5 collective-permute-start.5
  29.7 2.8 %collective-permute-done.6.refs_7_.refs_3_ = bf16[416,384]{1,0:T(8,128)(2,1)S(1)} collective-permute-done((bf16[416,384]{1,0:T(8,128)(2,1)S(1)}, bf16[416,384]{1,0:T(8,128)(2,1)S(1)}, u32[]{:S(2)}, u32[]{:S(2)}) %collective-permute-start.6) | collective-permute-done | bytes 319520 | tf_op jit(solution)/shard_map/ppermute | solution.py:454
  32.5 1.0 %collective-permute-start.11 = (bf16[816,384]{1,0:T(8,128)(2,1)S(1)}, bf16[816,384]{1,0:T(8,128)(2,1)S(1)}, u32[]{:S(2)}, u32[]{:S(2)}) collective-permute-start(bf16[816,384]{1,0:T(8,128)(2,1)S(1)} %get-tuple-element.65), channel_id=1, source_target_pairs={{0,2},{1,3},{2,0},{3,1},{4,6},{5,7},{6,4},{7,5},{8,10},{9,11},{10,... | collective-permute-start | bytes 1880072 | tf_op jit(solution)/shard_map/ppermute | solution.py:454
  33.5 1.0 %collective-permute-start.12 = (bf16[816,384]{1,0:T(8,128)(2,1)S(1)}, bf16[816,384]{1,0:T(8,128)(2,1)S(1)}, u32[]{:S(2)}, u32[]{:S(2)}) collective-permute-start(bf16[816,384]{1,0:T(8,128)(2,1)S(1)} %get-tuple-element.66), channel_id=1, source_target_pairs={{0,4},{1,5},{2,6},{3,7},{4,0},{5,1},{6,2},{7,3},{8,12},{9,13},{10,... | collective-permute-start | bytes 1880072 | tf_op jit(solution)/shard_map/ppermute | solution.py:454
  34.5 8.6 %first.1 = (bf16[2,1536,1536]{2,1,0:T(8,128)(2,1)S(1)}, f32[384,1536]{1,0:T(8,128)S(1)}, bf16[384,1536]{1,0:T(8,128)(2,1)S(1)}, f8e5m2[384,1536]{1,0:T(32,128)(4,1)S(1)}) custom-call(s32[1]{0:T(128)} %bitcast.idx_ref, f32[2,1536]{1,0:T(2,128)S(1)} %get-tuple-element.40.refs_3_.hop_ref, f32[2,1536,128]{2,1,0:T(8,128)S(1)} %get-tuple-element.38.down_ref, ...), custom_call_target="tpu_custom_call" | custom-call | tf_op jit(solution)/shard_map/first/pallas_call | solution.py:483
  43.2 0.1 collective-permute-start.9
  43.3 0.5 collective-permute-start.10
  43.8 1.4 %collective-permute-start.13 = (bf16[208,384]{1,0:T(8,128)(2,1)S(1)}, bf16[208,384]{1,0:T(8,128)(2,1)S(1)}, u32[]{:S(2)}, u32[]{:S(2)}) collective-permute-start(bf16[208,384]{1,0:T(8,128)(2,1)S(1)} %get-tuple-element.67), channel_id=1, source_target_pairs={{0,6},{1,7},{2,4},{3,5},{4,2},{5,3},{6,0},{7,1},{8,14},{9,15},{10,... | collective-permute-start | bytes 479240 | tf_op jit(solution)/shard_map/ppermute | solution.py:454
  45.2 0.1 collective-permute-done.9.refs_3_
  45.3 0.9 %collective-permute-done.10.refs_5_ = bf16[800,384]{1,0:T(8,128)(2,1)S(1)} collective-permute-done((bf16[800,384]{1,0:T(8,128)(2,1)S(1)}, bf16[800,384]{1,0:T(8,128)(2,1)S(1)}, u32[]{:S(2)}, u32[]{:S(2)}) %collective-permute-start.10) | collective-permute-done | bytes 614432 | tf_op jit(solution)/shard_map/ppermute | solution.py:454
  46.2 11.4 %second.1 = (bf16[384,1536]{1,0:T(8,128)(2,1)S(1)}, bf16[384,1536]{1,0:T(8,128)(2,1)S(1)}, f8e5m2[384,1536]{1,0:T(32,128)(4,1)S(1)}) custom-call(s32[1]{0:T(128)} %bitcast.idx_ref, bf16[384,1536]{1,0:T(8,128)(2,1)S(1)} %get-tuple-element.39.s1_ref, bf16[384,1536]{1,0:T(8,128)(2,1)S(1)} %get-tuple-element.51.refs_2_.w_hi, ...), custom_call_target="tpu_custom_call" | custom-call | tf_op jit(solution)/shard_map/second/pallas_call | solution.py:483
  57.6 6.9 %third.1 = (bf16[384,1536]{1,0:T(8,128)(2,1)S(1)}, f8e5m2[384,1536]{1,0:T(32,128)(4,1)S(1)}) custom-call(bf16[384,1536]{1,0:T(8,128)(2,1)S(1)} %get-tuple-element.56.hi, f8e5m2[384,1536]{1,0:T(32,128)(4,1)S(1)} %get-tuple-element.57.lo, bf16[2,1536,1536]{2,1,0:T(8,128)(2,1)S(1)} %get-tuple-element.58.scaled, f32[384,1536]{1,0:T(8,128)S(1)} %get-tuple-element.59.x), custom_call_target="tpu_custom_call" | custom-call | tf_op jit(solution)/shard_map/third/pallas_call | solution.py:483
  64.5 0.2 collective-permute-start.14
  64.7 0.4 collective-permute-start.15
  65.1 0.1 collective-permute-start.16
  65.2 4.7 %green_1.1.g1 = f32[2,192,1536]{2,1,0:T(8,128)S(1)} custom-call(s32[1]{0:T(128)} %bitcast.idx_ref, bf16[384,1536]{1,0:T(8,128)(2,1)S(1)} %get-tuple-element.62.left, bf16[2,1536,1536]{2,1,0:T(8,128)(2,1)S(1)} %get-tuple-element.58.scaled, bf16[3,2,192,1536]{3,2,1,0:T(8,128)(2,1)S(1)} %copy-done.1), custom_call_target="tpu_custom_call" | custom-call | tf_op jit(solution)/shard_map/green_1/pallas_call | solution.py:483
  70.0 8.7 %green_0.1 = f32[2,2,192,1536]{3,2,1,0:T(8,128)} custom-call(s32[1]{0:T(128)} %bitcast.idx_ref, f32[2,1536,128]{2,1,0:T(8,128)S(1)} %get-tuple-element.38.down_ref, bf16[384,1536]{1,0:T(8,128)(2,1)S(1)} %get-tuple-element.60.refs_3_.hi, f8e5m2[384,1536]{1,0:T(32,128)(4,1)S(1)} %get-tuple-element.61.lo, f32[2,192,1536]{2,1,0:T(8,128)S(1)} %green_1.1.g1, ...), custom_call_target="tpu_custom_call" | custom-call | tf_op jit(solution)/shard_map/green_0/pallas_call | solution.py:483
  (27 shorter events, 0.1 us)
Async XLA Ops:
  0.0 11.0 %collective-permute-start = (bf16[3,2,192,1536]{3,2,1,0:T(8,128)(2,1)}, bf16[3,2,192,1536]{3,2,1,0:T(8,128)(2,1)S(1)}, u32[]{:S(2)}, u32[]{:S(2)}) collective-permute-start(bf16[3,2,192,1536]{3,2,1,0:T(8,128)(2,1)} %refs_0_.5), channel_id=1, source_target_pairs={{0,1},{1,0},{2,3},{3,2},{4,5},{5,4},{6,7},{7,6},{8,9},{9,8},{10,11... | collective-permute-start | bytes 10616840 | tf_op jit(solution)/shard_map/ppermute | solution.py:454
  0.5 2.0 %copy-start = (bf16[3,2,192,1536]{3,2,1,0:T(8,128)(2,1)S(1)}, bf16[3,2,192,1536]{3,2,1,0:T(8,128)(2,1)}, u32[]{:S(2)}) copy-start(bf16[3,2,192,1536]{3,2,1,0:T(8,128)(2,1)} %refs_0_.5) | copy-start | bytes 10616836
  3.3 25.3 %collective-permute-start.1 = (bf16[784,384]{1,0:T(8,128)(2,1)S(1)}, bf16[784,384]{1,0:T(8,128)(2,1)S(1)}, u32[]{:S(2)}, u32[]{:S(2)}) collective-permute-start(bf16[784,384]{1,0:T(8,128)(2,1)S(1)} %get-tuple-element.43), channel_id=1, source_target_pairs={{0,2},{1,3},{2,0},{3,1},{4,6},{5,7},{6,4},{7,5},{8,10},{9,11},{10,... | collective-permute-start | bytes 1806344 | tf_op jit(solution)/shard_map/ppermute | solution.py:454
  5.9 23.3 %collective-permute-start.2 = (bf16[784,384]{1,0:T(8,128)(2,1)S(1)}, bf16[784,384]{1,0:T(8,128)(2,1)S(1)}, u32[]{:S(2)}, u32[]{:S(2)}) collective-permute-start(bf16[784,384]{1,0:T(8,128)(2,1)S(1)} %get-tuple-element.44), channel_id=1, source_target_pairs={{0,4},{1,5},{2,6},{3,7},{4,0},{5,1},{6,2},{7,3},{8,12},{9,13},{10,... | collective-permute-start | bytes 1806344 | tf_op jit(solution)/shard_map/ppermute | solution.py:454
  7.4 21.2 %collective-permute-start.3 = (bf16[416,384]{1,0:T(8,128)(2,1)S(1)}, bf16[416,384]{1,0:T(8,128)(2,1)S(1)}, u32[]{:S(2)}, u32[]{:S(2)}) collective-permute-start(bf16[416,384]{1,0:T(8,128)(2,1)S(1)} %get-tuple-element.45), channel_id=1, source_target_pairs={{0,6},{1,7},{2,4},{3,5},{4,2},{5,3},{6,0},{7,1},{8,14},{9,15},{10,... | collective-permute-start | bytes 958472 | tf_op jit(solution)/shard_map/ppermute | solution.py:454
  7.4 5.9 %copy-start.2 = (s32[3,1536]{1,0:T(4,128)S(1)}, s32[3,1536]{1,0:T(4,128)}, u32[]{:S(2)}) copy-start(s32[3,1536]{1,0:T(4,128)} %regions_ref.1) | copy-start | bytes 55300
  8.1 5.2 %copy-start.1 = (bf16[3,2,192,1536]{3,2,1,0:T(8,128)(2,1)S(1)}, bf16[3,2,192,1536]{3,2,1,0:T(8,128)(2,1)}, u32[]{:S(2)}) copy-start(bf16[3,2,192,1536]{3,2,1,0:T(8,128)(2,1)} %refs_0_.5) | copy-start | bytes 10616836
  8.1 5.2 %copy-start.3 = (f32[16]{0:T(128)S(1)}, f32[16]{0:T(128)}, u32[]{:S(2)}) copy-start(f32[16]{0:T(128)} %grid_ref.1) | copy-start | bytes 196
  8.1 5.2 %copy-start.4 = (f32[3]{0:T(128)S(1)}, f32[3]{0:T(128)}, u32[]{:S(2)}) copy-start(f32[3]{0:T(128)} %mass_ref.1) | copy-start | bytes 40
  8.1 5.2 %copy-start.5 = (f32[3]{0:T(128)S(1)}, f32[3]{0:T(128)}, u32[]{:S(2)}) copy-start(f32[3]{0:T(128)} %alpha_ref.1) | copy-start | bytes 40
  8.1 35.0 %collective-permute-start.8 = (bf16[800,384]{1,0:T(8,128)(2,1)S(1)}, bf16[800,384]{1,0:T(8,128)(2,1)S(1)}, u32[]{:S(2)}, u32[]{:S(2)}) collective-permute-start(bf16[800,384]{1,0:T(8,128)(2,1)S(1)} %get-tuple-element.53), channel_id=1, source_target_pairs={{0,4},{1,5},{2,6},{3,7},{4,0},{5,1},{6,2},{7,3},{8,12},{9,13},{10,... | collective-permute-start | bytes 1843208 | tf_op jit(solution)/shard_map/ppermute | solution.py:454
  11.1 32.1 %collective-permute-start.7 = (bf16[800,384]{1,0:T(8,128)(2,1)S(1)}, bf16[800,384]{1,0:T(8,128)(2,1)S(1)}, u32[]{:S(2)}, u32[]{:S(2)}) collective-permute-start(bf16[800,384]{1,0:T(8,128)(2,1)S(1)} %get-tuple-element.47.refs_5_), channel_id=1, source_target_pairs={{0,2},{1,3},{2,0},{3,1},{4,6},{5,7},{6,4},{7,5},{8,10},{9,11},{10,... | collective-permute-start | bytes 1843208 | tf_op jit(solution)/shard_map/ppermute | solution.py:454
  29.1 4.4 %collective-permute-start.4 = (bf16[784,384]{1,0:T(8,128)(2,1)S(1)}, bf16[784,384]{1,0:T(8,128)(2,1)S(1)}, u32[]{:S(2)}, u32[]{:S(2)}) collective-permute-start(bf16[784,384]{1,0:T(8,128)(2,1)S(1)} %get-tuple-element.48.refs_2_), channel_id=1, source_target_pairs={{0,1},{1,0},{2,3},{3,2},{4,5},{5,4},{6,7},{7,6},{8,9},{9,8},{10,11... | collective-permute-start | bytes 1806344 | tf_op jit(solution)/shard_map/ppermute | solution.py:454
  29.1 5.4 %collective-permute-start.5 = (bf16[784,384]{1,0:T(8,128)(2,1)S(1)}, bf16[784,384]{1,0:T(8,128)(2,1)S(1)}, u32[]{:S(2)}, u32[]{:S(2)}) collective-permute-start(bf16[784,384]{1,0:T(8,128)(2,1)S(1)} %get-tuple-element.49.refs_4_), channel_id=1, source_target_pairs={{0,1},{1,0},{2,3},{3,2},{4,5},{5,4},{6,7},{7,6},{8,9},{9,8},{10,11... | collective-permute-start | bytes 1806344 | tf_op jit(solution)/shard_map/ppermute | solution.py:454
  29.7 2.8 %collective-permute-start.6 = (bf16[416,384]{1,0:T(8,128)(2,1)S(1)}, bf16[416,384]{1,0:T(8,128)(2,1)S(1)}, u32[]{:S(2)}, u32[]{:S(2)}) collective-permute-start(bf16[416,384]{1,0:T(8,128)(2,1)S(1)} %get-tuple-element.50.refs_6_), channel_id=1, source_target_pairs={{0,1},{1,0},{2,3},{3,2},{4,5},{5,4},{6,7},{7,6},{8,9},{9,8},{10,11... | collective-permute-start | bytes 958472 | tf_op jit(solution)/shard_map/ppermute | solution.py:454
  32.5 32.0 %collective-permute-start.11 = (bf16[816,384]{1,0:T(8,128)(2,1)S(1)}, bf16[816,384]{1,0:T(8,128)(2,1)S(1)}, u32[]{:S(2)}, u32[]{:S(2)}) collective-permute-start(bf16[816,384]{1,0:T(8,128)(2,1)S(1)} %get-tuple-element.65), channel_id=1, source_target_pairs={{0,2},{1,3},{2,0},{3,1},{4,6},{5,7},{6,4},{7,5},{8,10},{9,11},{10,... | collective-permute-start | bytes 1880072 | tf_op jit(solution)/shard_map/ppermute | solution.py:454
  33.5 31.0 %collective-permute-start.12 = (bf16[816,384]{1,0:T(8,128)(2,1)S(1)}, bf16[816,384]{1,0:T(8,128)(2,1)S(1)}, u32[]{:S(2)}, u32[]{:S(2)}) collective-permute-start(bf16[816,384]{1,0:T(8,128)(2,1)S(1)} %get-tuple-element.66), channel_id=1, source_target_pairs={{0,4},{1,5},{2,6},{3,7},{4,0},{5,1},{6,2},{7,3},{8,12},{9,13},{10,... | collective-permute-start | bytes 1880072 | tf_op jit(solution)/shard_map/ppermute | solution.py:454
  43.2 2.1 %collective-permute-start.9 = (bf16[800,384]{1,0:T(8,128)(2,1)S(1)}, bf16[800,384]{1,0:T(8,128)(2,1)S(1)}, u32[]{:S(2)}, u32[]{:S(2)}) collective-permute-start(bf16[800,384]{1,0:T(8,128)(2,1)S(1)} %get-tuple-element.54.refs_2_), channel_id=1, source_target_pairs={{0,1},{1,0},{2,3},{3,2},{4,5},{5,4},{6,7},{7,6},{8,9},{9,8},{10,11... | collective-permute-start | bytes 1843208 | tf_op jit(solution)/shard_map/ppermute | solution.py:454
  43.3 2.9 %collective-permute-start.10 = (bf16[800,384]{1,0:T(8,128)(2,1)S(1)}, bf16[800,384]{1,0:T(8,128)(2,1)S(1)}, u32[]{:S(2)}, u32[]{:S(2)}) collective-permute-start(bf16[800,384]{1,0:T(8,128)(2,1)S(1)} %get-tuple-element.55.refs_4_), channel_id=1, source_target_pairs={{0,1},{1,0},{2,3},{3,2},{4,5},{5,4},{6,7},{7,6},{8,9},{9,8},{10,11... | collective-permute-start | bytes 1843208 | tf_op jit(solution)/shard_map/ppermute | solution.py:454
  43.8 20.7 %collective-permute-start.13 = (bf16[208,384]{1,0:T(8,128)(2,1)S(1)}, bf16[208,384]{1,0:T(8,128)(2,1)S(1)}, u32[]{:S(2)}, u32[]{:S(2)}) collective-permute-start(bf16[208,384]{1,0:T(8,128)(2,1)S(1)} %get-tuple-element.67), channel_id=1, source_target_pairs={{0,6},{1,7},{2,4},{3,5},{4,2},{5,3},{6,0},{7,1},{8,14},{9,15},{10,... | collective-permute-start | bytes 479240 | tf_op jit(solution)/shard_map/ppermute | solution.py:454
  64.5 5.5 %collective-permute-start.14 = (bf16[816,384]{1,0:T(8,128)(2,1)S(1)}, bf16[816,384]{1,0:T(8,128)(2,1)S(1)}, u32[]{:S(2)}, u32[]{:S(2)}) collective-permute-start(bf16[816,384]{1,0:T(8,128)(2,1)S(1)} %get-tuple-element.68.refs_2_), channel_id=1, source_target_pairs={{0,1},{1,0},{2,3},{3,2},{4,5},{5,4},{6,7},{7,6},{8,9},{9,8},{10,11... | collective-permute-start | bytes 1880072 | tf_op jit(solution)/shard_map/ppermute | solution.py:454
  64.7 5.3 %collective-permute-start.15 = (bf16[816,384]{1,0:T(8,128)(2,1)S(1)}, bf16[816,384]{1,0:T(8,128)(2,1)S(1)}, u32[]{:S(2)}, u32[]{:S(2)}) collective-permute-start(bf16[816,384]{1,0:T(8,128)(2,1)S(1)} %get-tuple-element.69.refs_4_), channel_id=1, source_target_pairs={{0,1},{1,0},{2,3},{3,2},{4,5},{5,4},{6,7},{7,6},{8,9},{9,8},{10,11... | collective-permute-start | bytes 1880072 | tf_op jit(solution)/shard_map/ppermute | solution.py:454
  65.1 4.9 %collective-permute-start.16 = (bf16[208,384]{1,0:T(8,128)(2,1)S(1)}, bf16[208,384]{1,0:T(8,128)(2,1)S(1)}, u32[]{:S(2)}, u32[]{:S(2)}) collective-permute-start(bf16[208,384]{1,0:T(8,128)(2,1)S(1)} %get-tuple-element.70.refs_6_), channel_id=1, source_target_pairs={{0,1},{1,0},{2,3},{3,2},{4,5},{5,4},{6,7},{7,6},{8,9},{9,8},{10,11... | collective-permute-start | bytes 479240 | tf_op jit(solution)/shard_map/ppermute | solution.py:454

commit v2 on v1

--- a/solution.py
+++ b/solution.py
@@ -71,7 +71,8 @@
     return jnp.stack(blocks[::-1])
 
 
-TILE = 512
+TILE = 256
+WIDE = 512
 LIMITS = (16, 16, 22, 24, 20)
 
 
@@ -410,10 +411,10 @@
     chip, core = own_part(idx_ref)
     copies = Copies(sems)
     mine = start_own(s, chip, a_ref, 1, own, copies)
-    for t in range(0, s.size, TILE):
-        (parts,) = multiply([(left, None)], planes(scaled, slice(t, t + TILE)), s)
-        copies.wait(mine)
-        add_own(s, own, parts, t, TILE, g1)
+    copies.wait(mine)
+    for t in range(0, s.size, WIDE):
+        (parts,) = multiply([(left, None)], planes(scaled, slice(t, t + WIDE)), s)
+        add_own(s, own, parts, t, WIDE, g1)
 
 
 def add_own(s, own, parts, start, width, g_ref):
@@ -440,7 +441,7 @@
     copies.wait()
     send_out(s, chip, 0, s.size, g1, out_ref, 1, copies)
     complete(s, whole, diags)
-    width = TILE // 2
+    width = TILE
     for t in range(0, s.size, width):
         cols = slice(t, t + width)
         right = [scale_rows(plane, down_ref, 0) for plane in planes(whole, cols)]

time: 79.1 us -> 78 us (0.986)
  Pallas kernels: 44.3 us -> 43.3 us
    pallas_call x5, Pallas kernels: 40.3 us -> 39.3 us  [call(): pl.pallas_call(functools.partial(kernel, s), in_specs=[SMEM if x is idx e...]
  transfers between devices with their start and end apart: 17 -> 17, of which waited for: 5 -> 5; matrix products, arithmetic and copies ran while one was open for 0% -> 0% of each run, Pallas kernels for 45% -> 44%
where the time goes in v2:
time: 78 us; the launch traced here: 77.8 us
  Pallas kernels  43.3 us (56%)
  waiting for transfers between devices  18 us (23%)
  starting transfers between devices  13.4 us (17%)
  local copies, waits for them, and re-layouts  2.03 us (3%)
  between operations  1.07 us (1%)
    pallas_call x5, Pallas kernels, call(): pl.pallas_call(functools.partial(kernel, s), in_specs=[SMEM if x is idx e...  39.3 us
    ppermute x17, waiting for transfers between devices, swap(): return lax.ppermute(x, 'cols', [(i, i ^ mask) for i in range(n)])  18 us
    ppermute x17, starting transfers between devices, swap(): return lax.ppermute(x, 'cols', [(i, i ^ mask) for i in range(n)])  13.4 us
    pallas_call x3, Pallas kernels, pack(): pl.pallas_call(functools.partial(pack_kernel, s, index, heads), in_specs=...  2.37 us
    unnamed x12, local copies, waits for them, and re-layouts  2.03 us
    pallas_call x1, Pallas kernels, prep(): pl.pallas_call(functools.partial(prep_kernel, s), grid=(1,), in_specs=[SM...  1.61 us
  transfers between devices with their start and end apart: 17, of which 5 were waited for; matrix products, arithmetic and copies ran while one was open for 0% of the time, Pallas kernels for 44%

profile of v2, /device:TPU:0, one launch (start us, length us, event | category | flops | bytes accessed | tf_op | source)
XLA Modules:
  0.0 77.8 jit_solution(5964925270938525925)
XLA Ops:
  0.0 0.5 collective-permute-start
  0.5 2.0 %copy-done = bf16[3,2,192,1536]{3,2,1,0:T(8,128)(2,1)S(1)} copy-done((bf16[3,2,192,1536]{3,2,1,0:T(8,128)(2,1)S(1)}, bf16[3,2,192,1536]{3,2,1,0:T(8,128)(2,1)}, u32[]{:S(2)}) %copy-start) | copy-done | bytes 3538968
  2.5 0.8 %pack.3 = (bf16[784,384]{1,0:T(8,128)(2,1)S(1)}, bf16[784,384]{1,0:T(8,128)(2,1)S(1)}, bf16[416,384]{1,0:T(8,128)(2,1)S(1)}) custom-call(s32[1]{0:T(128)} %bitcast.idx_ref, bf16[3,2,192,1536]{3,2,1,0:T(8,128)(2,1)S(1)} %copy-done), custom_call_target="tpu_custom_call" | custom-call | tf_op jit(solution)/shard_map/pack/pallas_call | solution.py:165
  3.3 2.6 %collective-permute-start.1 = (bf16[784,384]{1,0:T(8,128)(2,1)S(1)}, bf16[784,384]{1,0:T(8,128)(2,1)S(1)}, u32[]{:S(2)}, u32[]{:S(2)}) collective-permute-start(bf16[784,384]{1,0:T(8,128)(2,1)S(1)} %get-tuple-element.43), channel_id=1, source_target_pairs={{0,2},{1,3},{2,0},{3,1},{4,6},{5,7},{6,4},{7,5},{8,10},{9,11},{10,... | collective-permute-start | bytes 1806344 | tf_op jit(solution)/shard_map/ppermute | solution.py:455
  5.9 1.5 %collective-permute-start.2 = (bf16[784,384]{1,0:T(8,128)(2,1)S(1)}, bf16[784,384]{1,0:T(8,128)(2,1)S(1)}, u32[]{:S(2)}, u32[]{:S(2)}) collective-permute-start(bf16[784,384]{1,0:T(8,128)(2,1)S(1)} %get-tuple-element.44), channel_id=1, source_target_pairs={{0,4},{1,5},{2,6},{3,7},{4,0},{5,1},{6,2},{7,3},{8,12},{9,13},{10,... | collective-permute-start | bytes 1806344 | tf_op jit(solution)/shard_map/ppermute | solution.py:455
  7.4 0.0 collective-permute-start.3
  7.4 0.6 pack.5
  8.1 0.0 copy-start.1
  8.1 0.0 copy-start.5
  8.1 2.0 %collective-permute-start.8 = (bf16[800,384]{1,0:T(8,128)(2,1)S(1)}, bf16[800,384]{1,0:T(8,128)(2,1)S(1)}, u32[]{:S(2)}, u32[]{:S(2)}) collective-permute-start(bf16[800,384]{1,0:T(8,128)(2,1)S(1)} %get-tuple-element.53), channel_id=1, source_target_pairs={{0,4},{1,5},{2,6},{3,7},{4,0},{5,1},{6,2},{7,3},{8,12},{9,13},{10,... | collective-permute-start | bytes 1843208 | tf_op jit(solution)/shard_map/ppermute | solution.py:455
  10.2 0.9 %pack.4 = (bf16[816,384]{1,0:T(8,128)(2,1)S(1)}, bf16[816,384]{1,0:T(8,128)(2,1)S(1)}, bf16[208,384]{1,0:T(8,128)(2,1)S(1)}) custom-call(s32[1]{0:T(128)} %bitcast.idx_ref, bf16[3,2,192,1536]{3,2,1,0:T(8,128)(2,1)S(1)} %copy-done), custom_call_target="tpu_custom_call" | custom-call | tf_op jit(solution)/shard_map/pack/pallas_call | solution.py:165
  11.1 1.6 %collective-permute-start.7 = (bf16[800,384]{1,0:T(8,128)(2,1)S(1)}, bf16[800,384]{1,0:T(8,128)(2,1)S(1)}, u32[]{:S(2)}, u32[]{:S(2)}) collective-permute-start(bf16[800,384]{1,0:T(8,128)(2,1)S(1)} %get-tuple-element.47.refs_5_), channel_id=1, source_target_pairs={{0,2},{1,3},{2,0},{3,1},{4,6},{5,7},{6,4},{7,5},{8,10},{9,11},{10,... | collective-permute-start | bytes 1843208 | tf_op jit(solution)/shard_map/ppermute | solution.py:455
  13.3 1.6 %prep.1 = (f32[2,1536]{1,0:T(2,128)S(1)}, f32[2,1536,128]{2,1,0:T(8,128)S(1)}, bf16[384,1536]{1,0:T(8,128)(2,1)S(1)}, f8e5m2[384,1536]{1,0:T(32,128)(4,1)S(1)}, bf16[384,1536]{1,0:T(8,128)(2,1)S(1)}) custom-call(s32[1]{0:T(128)} %bitcast.idx_ref, s32[1]{0:T(128)S(6)} %copy.29.index_ref, f32[16]{0:T(128)S(1)} %copy-done.3, f32[3]{0:T(128)S(1)} %copy-done.4, ...), custom_call_target="tpu_custom_call" | custom-call | tf_op jit(solution)/shard_map/prep/pallas_call | solution.py:243
  14.9 13.7 %collective-permute-done.3.refs_2_ = bf16[416,384]{1,0:T(8,128)(2,1)S(1)} collective-permute-done((bf16[416,384]{1,0:T(8,128)(2,1)S(1)}, bf16[416,384]{1,0:T(8,128)(2,1)S(1)}, u32[]{:S(2)}, u32[]{:S(2)}) %collective-permute-start.3) | collective-permute-done | bytes 319520 | tf_op jit(solution)/shard_map/ppermute | solution.py:455
  28.6 0.5 collective-permute-done.2.refs_1_
  29.1 0.5 collective-permute-start.5
  29.7 2.8 %collective-permute-done.6.refs_7_.refs_3_ = bf16[416,384]{1,0:T(8,128)(2,1)S(1)} collective-permute-done((bf16[416,384]{1,0:T(8,128)(2,1)S(1)}, bf16[416,384]{1,0:T(8,128)(2,1)S(1)}, u32[]{:S(2)}, u32[]{:S(2)}) %collective-permute-start.6) | collective-permute-done | bytes 319520 | tf_op jit(solution)/shard_map/ppermute | solution.py:455
  32.5 1.0 %collective-permute-start.11 = (bf16[816,384]{1,0:T(8,128)(2,1)S(1)}, bf16[816,384]{1,0:T(8,128)(2,1)S(1)}, u32[]{:S(2)}, u32[]{:S(2)}) collective-permute-start(bf16[816,384]{1,0:T(8,128)(2,1)S(1)} %get-tuple-element.65), channel_id=1, source_target_pairs={{0,2},{1,3},{2,0},{3,1},{4,6},{5,7},{6,4},{7,5},{8,10},{9,11},{10,... | collective-permute-start | bytes 1880072 | tf_op jit(solution)/shard_map/ppermute | solution.py:455
  33.5 1.0 %collective-permute-start.12 = (bf16[816,384]{1,0:T(8,128)(2,1)S(1)}, bf16[816,384]{1,0:T(8,128)(2,1)S(1)}, u32[]{:S(2)}, u32[]{:S(2)}) collective-permute-start(bf16[816,384]{1,0:T(8,128)(2,1)S(1)} %get-tuple-element.66), channel_id=1, source_target_pairs={{0,4},{1,5},{2,6},{3,7},{4,0},{5,1},{6,2},{7,3},{8,12},{9,13},{10,... | collective-permute-start | bytes 1880072 | tf_op jit(solution)/shard_map/ppermute | solution.py:455
  34.5 8.7 %first.1 = (bf16[2,1536,1536]{2,1,0:T(8,128)(2,1)S(1)}, f32[384,1536]{1,0:T(8,128)S(1)}, bf16[384,1536]{1,0:T(8,128)(2,1)S(1)}, f8e5m2[384,1536]{1,0:T(32,128)(4,1)S(1)}) custom-call(s32[1]{0:T(128)} %bitcast.idx_ref, f32[2,1536]{1,0:T(2,128)S(1)} %get-tuple-element.40.refs_3_.hop_ref, f32[2,1536,128]{2,1,0:T(8,128)S(1)} %get-tuple-element.38.down_ref, ...), custom_call_target="tpu_custom_call" | custom-call | tf_op jit(solution)/shard_map/first/pallas_call | solution.py:484
  43.3 0.1 collective-permute-start.9
  43.3 0.5 collective-permute-start.10
  43.8 1.4 %collective-permute-start.13 = (bf16[208,384]{1,0:T(8,128)(2,1)S(1)}, bf16[208,384]{1,0:T(8,128)(2,1)S(1)}, u32[]{:S(2)}, u32[]{:S(2)}) collective-permute-start(bf16[208,384]{1,0:T(8,128)(2,1)S(1)} %get-tuple-element.67), channel_id=1, source_target_pairs={{0,6},{1,7},{2,4},{3,5},{4,2},{5,3},{6,0},{7,1},{8,14},{9,15},{10,... | collective-permute-start | bytes 479240 | tf_op jit(solution)/shard_map/ppermute | solution.py:455
  45.3 0.1 collective-permute-done.9.refs_3_
  45.4 0.9 %collective-permute-done.10.refs_5_ = bf16[800,384]{1,0:T(8,128)(2,1)S(1)} collective-permute-done((bf16[800,384]{1,0:T(8,128)(2,1)S(1)}, bf16[800,384]{1,0:T(8,128)(2,1)S(1)}, u32[]{:S(2)}, u32[]{:S(2)}) %collective-permute-start.10) | collective-permute-done | bytes 614432 | tf_op jit(solution)/shard_map/ppermute | solution.py:455
  46.2 11.0 %second.1 = (bf16[384,1536]{1,0:T(8,128)(2,1)S(1)}, bf16[384,1536]{1,0:T(8,128)(2,1)S(1)}, f8e5m2[384,1536]{1,0:T(32,128)(4,1)S(1)}) custom-call(s32[1]{0:T(128)} %bitcast.idx_ref, bf16[384,1536]{1,0:T(8,128)(2,1)S(1)} %get-tuple-element.39.s1_ref, bf16[384,1536]{1,0:T(8,128)(2,1)S(1)} %get-tuple-element.51.refs_2_.w_hi, ...), custom_call_target="tpu_custom_call" | custom-call | tf_op jit(solution)/shard_map/second/pallas_call | solution.py:484
  57.2 6.4 %third.1 = (bf16[384,1536]{1,0:T(8,128)(2,1)S(1)}, f8e5m2[384,1536]{1,0:T(32,128)(4,1)S(1)}) custom-call(bf16[384,1536]{1,0:T(8,128)(2,1)S(1)} %get-tuple-element.56.hi, f8e5m2[384,1536]{1,0:T(32,128)(4,1)S(1)} %get-tuple-element.57.lo, bf16[2,1536,1536]{2,1,0:T(8,128)(2,1)S(1)} %get-tuple-element.58.scaled, f32[384,1536]{1,0:T(8,128)S(1)} %get-tuple-element.59.x), custom_call_target="tpu_custom_call" | custom-call | tf_op jit(solution)/shard_map/third/pallas_call | solution.py:484
  63.7 0.2 collective-permute-start.14
  63.9 0.4 collective-permute-start.15
  64.3 0.1 collective-permute-start.16
  64.4 4.5 %green_1.1.g1 = f32[2,192,1536]{2,1,0:T(8,128)S(1)} custom-call(s32[1]{0:T(128)} %bitcast.idx_ref, bf16[384,1536]{1,0:T(8,128)(2,1)S(1)} %get-tuple-element.62.left, bf16[2,1536,1536]{2,1,0:T(8,128)(2,1)S(1)} %get-tuple-element.58.scaled, bf16[3,2,192,1536]{3,2,1,0:T(8,128)(2,1)S(1)} %copy-done.1), custom_call_target="tpu_custom_call" | custom-call | tf_op jit(solution)/shard_map/green_1/pallas_call | solution.py:484
  68.9 8.7 %green_0.1 = f32[2,2,192,1536]{3,2,1,0:T(8,128)} custom-call(s32[1]{0:T(128)} %bitcast.idx_ref, f32[2,1536,128]{2,1,0:T(8,128)S(1)} %get-tuple-element.38.down_ref, bf16[384,1536]{1,0:T(8,128)(2,1)S(1)} %get-tuple-element.60.refs_3_.hi, f8e5m2[384,1536]{1,0:T(32,128)(4,1)S(1)} %get-tuple-element.61.lo, f32[2,192,1536]{2,1,0:T(8,128)S(1)} %green_1.1.g1, ...), custom_call_target="tpu_custom_call" | custom-call | tf_op jit(solution)/shard_map/green_0/pallas_call | solution.py:484
  (27 shorter events, 0.1 us)
Async XLA Ops:
  0.0 11.0 %collective-permute-start = (bf16[3,2,192,1536]{3,2,1,0:T(8,128)(2,1)}, bf16[3,2,192,1536]{3,2,1,0:T(8,128)(2,1)S(1)}, u32[]{:S(2)}, u32[]{:S(2)}) collective-permute-start(bf16[3,2,192,1536]{3,2,1,0:T(8,128)(2,1)} %refs_0_.5), channel_id=1, source_target_pairs={{0,1},{1,0},{2,3},{3,2},{4,5},{5,4},{6,7},{7,6},{8,9},{9,8},{10,11... | collective-permute-start | bytes 10616840 | tf_op jit(solution)/shard_map/ppermute | solution.py:455
  0.5 2.0 %copy-start = (bf16[3,2,192,1536]{3,2,1,0:T(8,128)(2,1)S(1)}, bf16[3,2,192,1536]{3,2,1,0:T(8,128)(2,1)}, u32[]{:S(2)}) copy-start(bf16[3,2,192,1536]{3,2,1,0:T(8,128)(2,1)} %refs_0_.5) | copy-start | bytes 10616836
  3.3 25.3 %collective-permute-start.1 = (bf16[784,384]{1,0:T(8,128)(2,1)S(1)}, bf16[784,384]{1,0:T(8,128)(2,1)S(1)}, u32[]{:S(2)}, u32[]{:S(2)}) collective-permute-start(bf16[784,384]{1,0:T(8,128)(2,1)S(1)} %get-tuple-element.43), channel_id=1, source_target_pairs={{0,2},{1,3},{2,0},{3,1},{4,6},{5,7},{6,4},{7,5},{8,10},{9,11},{10,... | collective-permute-start | bytes 1806344 | tf_op jit(solution)/shard_map/ppermute | solution.py:455
  5.9 23.3 %collective-permute-start.2 = (bf16[784,384]{1,0:T(8,128)(2,1)S(1)}, bf16[784,384]{1,0:T(8,128)(2,1)S(1)}, u32[]{:S(2)}, u32[]{:S(2)}) collective-permute-start(bf16[784,384]{1,0:T(8,128)(2,1)S(1)} %get-tuple-element.44), channel_id=1, source_target_pairs={{0,4},{1,5},{2,6},{3,7},{4,0},{5,1},{6,2},{7,3},{8,12},{9,13},{10,... | collective-permute-start | bytes 1806344 | tf_op jit(solution)/shard_map/ppermute | solution.py:455
  7.4 21.2 %collective-permute-start.3 = (bf16[416,384]{1,0:T(8,128)(2,1)S(1)}, bf16[416,384]{1,0:T(8,128)(2,1)S(1)}, u32[]{:S(2)}, u32[]{:S(2)}) collective-permute-start(bf16[416,384]{1,0:T(8,128)(2,1)S(1)} %get-tuple-element.45), channel_id=1, source_target_pairs={{0,6},{1,7},{2,4},{3,5},{4,2},{5,3},{6,0},{7,1},{8,14},{9,15},{10,... | collective-permute-start | bytes 958472 | tf_op jit(solution)/shard_map/ppermute | solution.py:455
  7.4 5.9 %copy-start.2 = (s32[3,1536]{1,0:T(4,128)S(1)}, s32[3,1536]{1,0:T(4,128)}, u32[]{:S(2)}) copy-start(s32[3,1536]{1,0:T(4,128)} %regions_ref.1) | copy-start | bytes 55300
  8.1 5.2 %copy-start.1 = (bf16[3,2,192,1536]{3,2,1,0:T(8,128)(2,1)S(1)}, bf16[3,2,192,1536]{3,2,1,0:T(8,128)(2,1)}, u32[]{:S(2)}) copy-start(bf16[3,2,192,1536]{3,2,1,0:T(8,128)(2,1)} %refs_0_.5) | copy-start | bytes 10616836
  8.1 5.2 %copy-start.3 = (f32[16]{0:T(128)S(1)}, f32[16]{0:T(128)}, u32[]{:S(2)}) copy-start(f32[16]{0:T(128)} %grid_ref.1) | copy-start | bytes 196
  8.1 5.2 %copy-start.4 = (f32[3]{0:T(128)S(1)}, f32[3]{0:T(128)}, u32[]{:S(2)}) copy-start(f32[3]{0:T(128)} %mass_ref.1) | copy-start | bytes 40
  8.1 5.2 %copy-start.5 = (f32[3]{0:T(128)S(1)}, f32[3]{0:T(128)}, u32[]{:S(2)}) copy-start(f32[3]{0:T(128)} %alpha_ref.1) | copy-start | bytes 40
  8.1 35.1 %collective-permute-start.8 = (bf16[800,384]{1,0:T(8,128)(2,1)S(1)}, bf16[800,384]{1,0:T(8,128)(2,1)S(1)}, u32[]{:S(2)}, u32[]{:S(2)}) collective-permute-start(bf16[800,384]{1,0:T(8,128)(2,1)S(1)} %get-tuple-element.53), channel_id=1, source_target_pairs={{0,4},{1,5},{2,6},{3,7},{4,0},{5,1},{6,2},{7,3},{8,12},{9,13},{10,... | collective-permute-start | bytes 1843208 | tf_op jit(solution)/shard_map/ppermute | solution.py:455
  11.1 32.2 %collective-permute-start.7 = (bf16[800,384]{1,0:T(8,128)(2,1)S(1)}, bf16[800,384]{1,0:T(8,128)(2,1)S(1)}, u32[]{:S(2)}, u32[]{:S(2)}) collective-permute-start(bf16[800,384]{1,0:T(8,128)(2,1)S(1)} %get-tuple-element.47.refs_5_), channel_id=1, source_target_pairs={{0,2},{1,3},{2,0},{3,1},{4,6},{5,7},{6,4},{7,5},{8,10},{9,11},{10,... | collective-permute-start | bytes 1843208 | tf_op jit(solution)/shard_map/ppermute | solution.py:455
  29.1 4.4 %collective-permute-start.4 = (bf16[784,384]{1,0:T(8,128)(2,1)S(1)}, bf16[784,384]{1,0:T(8,128)(2,1)S(1)}, u32[]{:S(2)}, u32[]{:S(2)}) collective-permute-start(bf16[784,384]{1,0:T(8,128)(2,1)S(1)} %get-tuple-element.48.refs_2_), channel_id=1, source_target_pairs={{0,1},{1,0},{2,3},{3,2},{4,5},{5,4},{6,7},{7,6},{8,9},{9,8},{10,11... | collective-permute-start | bytes 1806344 | tf_op jit(solution)/shard_map/ppermute | solution.py:455
  29.1 5.4 %collective-permute-start.5 = (bf16[784,384]{1,0:T(8,128)(2,1)S(1)}, bf16[784,384]{1,0:T(8,128)(2,1)S(1)}, u32[]{:S(2)}, u32[]{:S(2)}) collective-permute-start(bf16[784,384]{1,0:T(8,128)(2,1)S(1)} %get-tuple-element.49.refs_4_), channel_id=1, source_target_pairs={{0,1},{1,0},{2,3},{3,2},{4,5},{5,4},{6,7},{7,6},{8,9},{9,8},{10,11... | collective-permute-start | bytes 1806344 | tf_op jit(solution)/shard_map/ppermute | solution.py:455
  29.7 2.8 %collective-permute-start.6 = (bf16[416,384]{1,0:T(8,128)(2,1)S(1)}, bf16[416,384]{1,0:T(8,128)(2,1)S(1)}, u32[]{:S(2)}, u32[]{:S(2)}) collective-permute-start(bf16[416,384]{1,0:T(8,128)(2,1)S(1)} %get-tuple-element.50.refs_6_), channel_id=1, source_target_pairs={{0,1},{1,0},{2,3},{3,2},{4,5},{5,4},{6,7},{7,6},{8,9},{9,8},{10,11... | collective-permute-start | bytes 958472 | tf_op jit(solution)/shard_map/ppermute | solution.py:455
  32.5 31.2 %collective-permute-start.11 = (bf16[816,384]{1,0:T(8,128)(2,1)S(1)}, bf16[816,384]{1,0:T(8,128)(2,1)S(1)}, u32[]{:S(2)}, u32[]{:S(2)}) collective-permute-start(bf16[816,384]{1,0:T(8,128)(2,1)S(1)} %get-tuple-element.65), channel_id=1, source_target_pairs={{0,2},{1,3},{2,0},{3,1},{4,6},{5,7},{6,4},{7,5},{8,10},{9,11},{10,... | collective-permute-start | bytes 1880072 | tf_op jit(solution)/shard_map/ppermute | solution.py:455
  33.5 30.2 %collective-permute-start.12 = (bf16[816,384]{1,0:T(8,128)(2,1)S(1)}, bf16[816,384]{1,0:T(8,128)(2,1)S(1)}, u32[]{:S(2)}, u32[]{:S(2)}) collective-permute-start(bf16[816,384]{1,0:T(8,128)(2,1)S(1)} %get-tuple-element.66), channel_id=1, source_target_pairs={{0,4},{1,5},{2,6},{3,7},{4,0},{5,1},{6,2},{7,3},{8,12},{9,13},{10,... | collective-permute-start | bytes 1880072 | tf_op jit(solution)/shard_map/ppermute | solution.py:455
  43.3 2.1 %collective-permute-start.9 = (bf16[800,384]{1,0:T(8,128)(2,1)S(1)}, bf16[800,384]{1,0:T(8,128)(2,1)S(1)}, u32[]{:S(2)}, u32[]{:S(2)}) collective-permute-start(bf16[800,384]{1,0:T(8,128)(2,1)S(1)} %get-tuple-element.54.refs_2_), channel_id=1, source_target_pairs={{0,1},{1,0},{2,3},{3,2},{4,5},{5,4},{6,7},{7,6},{8,9},{9,8},{10,11... | collective-permute-start | bytes 1843208 | tf_op jit(solution)/shard_map/ppermute | solution.py:455
  43.3 2.9 %collective-permute-start.10 = (bf16[800,384]{1,0:T(8,128)(2,1)S(1)}, bf16[800,384]{1,0:T(8,128)(2,1)S(1)}, u32[]{:S(2)}, u32[]{:S(2)}) collective-permute-start(bf16[800,384]{1,0:T(8,128)(2,1)S(1)} %get-tuple-element.55.refs_4_), channel_id=1, source_target_pairs={{0,1},{1,0},{2,3},{3,2},{4,5},{5,4},{6,7},{7,6},{8,9},{9,8},{10,11... | collective-permute-start | bytes 1843208 | tf_op jit(solution)/shard_map/ppermute | solution.py:455
  43.8 19.8 %collective-permute-start.13 = (bf16[208,384]{1,0:T(8,128)(2,1)S(1)}, bf16[208,384]{1,0:T(8,128)(2,1)S(1)}, u32[]{:S(2)}, u32[]{:S(2)}) collective-permute-start(bf16[208,384]{1,0:T(8,128)(2,1)S(1)} %get-tuple-element.67), channel_id=1, source_target_pairs={{0,6},{1,7},{2,4},{3,5},{4,2},{5,3},{6,0},{7,1},{8,14},{9,15},{10,... | collective-permute-start | bytes 479240 | tf_op jit(solution)/shard_map/ppermute | solution.py:455
  63.7 5.2 %collective-permute-start.14 = (bf16[816,384]{1,0:T(8,128)(2,1)S(1)}, bf16[816,384]{1,0:T(8,128)(2,1)S(1)}, u32[]{:S(2)}, u32[]{:S(2)}) collective-permute-start(bf16[816,384]{1,0:T(8,128)(2,1)S(1)} %get-tuple-element.68.refs_2_), channel_id=1, source_target_pairs={{0,1},{1,0},{2,3},{3,2},{4,5},{5,4},{6,7},{7,6},{8,9},{9,8},{10,11... | collective-permute-start | bytes 1880072 | tf_op jit(solution)/shard_map/ppermute | solution.py:455
  63.9 5.0 %collective-permute-start.15 = (bf16[816,384]{1,0:T(8,128)(2,1)S(1)}, bf16[816,384]{1,0:T(8,128)(2,1)S(1)}, u32[]{:S(2)}, u32[]{:S(2)}) collective-permute-start(bf16[816,384]{1,0:T(8,128)(2,1)S(1)} %get-tuple-element.69.refs_4_), channel_id=1, source_target_pairs={{0,1},{1,0},{2,3},{3,2},{4,5},{5,4},{6,7},{7,6},{8,9},{9,8},{10,11... | collective-permute-start | bytes 1880072 | tf_op jit(solution)/shard_map/ppermute | solution.py:455
  64.3 4.6 %collective-permute-start.16 = (bf16[208,384]{1,0:T(8,128)(2,1)S(1)}, bf16[208,384]{1,0:T(8,128)(2,1)S(1)}, u32[]{:S(2)}, u32[]{:S(2)}) collective-permute-start(bf16[208,384]{1,0:T(8,128)(2,1)S(1)} %get-tuple-element.70.refs_6_), channel_id=1, source_target_pairs={{0,1},{1,0},{2,3},{3,2},{4,5},{5,4},{6,7},{7,6},{8,9},{9,8},{10,11... | collective-permute-start | bytes 479240 | tf_op jit(solution)/shard_map/ppermute | solution.py:455

commit v3 on v2

--- a/solution.py
+++ b/solution.py
@@ -51,23 +51,20 @@
 
 def general(left_inverse, regions, region_mass, region_alpha, energy_grid, energy_index):
     hop = couplings(regions, region_mass, region_alpha, energy_grid, energy_index)
-    count = left_inverse.shape[0]
-    whole = [None] * count
-    for index in list(range(count - 2, -1, -1)) + [count - 1]:
-        whole[index] = lax.all_gather(left_inverse[index], "cols", axis=1, tiled=True)
+    count, _, own_rows, _ = left_inverse.shape
+    offset = lax.axis_index("cols") * own_rows
+    own_hop = lax.dynamic_slice_in_dim(hop, offset, own_rows, 1)
+    whole = [lax.all_gather(a, "cols", axis=1, tiled=True) for a in left_inverse[: count - 1]]
+    next_green = left_inverse[count - 1]
     blocks = []
     for index in range(count - 2, -1, -1):
-        rows = left_inverse[index].astype(F32)
-
-        def times_green(left, level):
-            if level == count - 1:
-                return product(left, whole[level])
-            first = product(left, whole[level])
-            inner = times_green((first * hop[level]).astype(BF16), level + 1)
-            return first + product((inner * hop[level]).astype(BF16), whole[level])
-
-        inner = times_green((rows * hop[index]).astype(BF16), index + 1)
-        blocks.append(rows + product((inner * hop[index]).astype(BF16), whole[index]))
+        panel = left_inverse[index]
+        scaled = (hop[index][None, :, None] * whole[index].astype(F32)).astype(BF16)
+        image = (own_hop[index][None, :, None] * product(next_green, scaled)).astype(BF16)
+        image = lax.all_gather(image, "cols", axis=1, tiled=True)
+        current = panel.astype(F32) + product(panel, image)
+        blocks.append(current)
+        next_green = current.astype(BF16)
     return jnp.stack(blocks[::-1])
 
 
@@ -503,7 +500,7 @@
         [whole, diags, sems],
         LIMITS[1],
     )
-    x0, y0, z0 = gate([x0, y0, z0], (z_cross,))
+    x0, y0, z0 = gate([x0, y0, z0], (w_hi,))
     x0, y0, z0 = swap(x0, 2), swap(y0, 4), swap(z0, 6)
     x2, y2 = gate([x2, y2], (w_hi,))
     u, y_hi, y_lo = call(

time: 78 us -> 77.8 us (level)
  no operation moved by 1% of the time
where the time goes in v3:
time: 77.8 us; the launch traced here: 77.7 us
  Pallas kernels  43.1 us (55%)
  waiting for transfers between devices  18.1 us (23%)
  starting transfers between devices  13.4 us (17%)
  local copies, waits for them, and re-layouts  2.03 us (3%)
  between operations  1.02 us (1%)
    pallas_call x5, Pallas kernels, call(): pl.pallas_call(functools.partial(kernel, s), in_specs=[SMEM if x is idx e...  39.1 us
    ppermute x17, waiting for transfers between devices, swap(): return lax.ppermute(x, 'cols', [(i, i ^ mask) for i in range(n)])  18.1 us
    ppermute x17, starting transfers between devices, swap(): return lax.ppermute(x, 'cols', [(i, i ^ mask) for i in range(n)])  13.4 us
    pallas_call x3, Pallas kernels, pack(): pl.pallas_call(functools.partial(pack_kernel, s, index, heads), in_specs=...  2.37 us
    unnamed x12, local copies, waits for them, and re-layouts  2.03 us
    pallas_call x1, Pallas kernels, prep(): pl.pallas_call(functools.partial(prep_kernel, s), grid=(1,), in_specs=[SM...  1.61 us
  transfers between devices with their start and end apart: 17, of which 5 were waited for; matrix products, arithmetic and copies ran while one was open for 0% of the time, Pallas kernels for 44%

profile of v3, /device:TPU:0, one launch (start us, length us, event | category | flops | bytes accessed | tf_op | source)
XLA Modules:
  0.0 77.7 jit_solution(14296457171037727903)
XLA Ops:
  0.0 0.5 collective-permute-start
  0.5 2.0 %copy-done = bf16[3,2,192,1536]{3,2,1,0:T(8,128)(2,1)S(1)} copy-done((bf16[3,2,192,1536]{3,2,1,0:T(8,128)(2,1)S(1)}, bf16[3,2,192,1536]{3,2,1,0:T(8,128)(2,1)}, u32[]{:S(2)}) %copy-start) | copy-done | bytes 3538968
  2.5 0.8 %pack.3 = (bf16[784,384]{1,0:T(8,128)(2,1)S(1)}, bf16[784,384]{1,0:T(8,128)(2,1)S(1)}, bf16[416,384]{1,0:T(8,128)(2,1)S(1)}) custom-call(s32[1]{0:T(128)} %bitcast.idx_ref, bf16[3,2,192,1536]{3,2,1,0:T(8,128)(2,1)S(1)} %copy-done), custom_call_target="tpu_custom_call" | custom-call | tf_op jit(solution)/shard_map/pack/pallas_call | solution.py:162
  3.3 2.6 %collective-permute-start.1 = (bf16[784,384]{1,0:T(8,128)(2,1)S(1)}, bf16[784,384]{1,0:T(8,128)(2,1)S(1)}, u32[]{:S(2)}, u32[]{:S(2)}) collective-permute-start(bf16[784,384]{1,0:T(8,128)(2,1)S(1)} %get-tuple-element.43), channel_id=1, source_target_pairs={{0,2},{1,3},{2,0},{3,1},{4,6},{5,7},{6,4},{7,5},{8,10},{9,11},{10,... | collective-permute-start | bytes 1806344 | tf_op jit(solution)/shard_map/ppermute | solution.py:452
  5.9 1.5 %collective-permute-start.2 = (bf16[784,384]{1,0:T(8,128)(2,1)S(1)}, bf16[784,384]{1,0:T(8,128)(2,1)S(1)}, u32[]{:S(2)}, u32[]{:S(2)}) collective-permute-start(bf16[784,384]{1,0:T(8,128)(2,1)S(1)} %get-tuple-element.44), channel_id=1, source_target_pairs={{0,4},{1,5},{2,6},{3,7},{4,0},{5,1},{6,2},{7,3},{8,12},{9,13},{10,... | collective-permute-start | bytes 1806344 | tf_op jit(solution)/shard_map/ppermute | solution.py:452
  7.4 0.0 collective-permute-start.3
  7.4 0.6 pack.5
  8.1 0.0 copy-start.1
  8.1 0.0 copy-start.3
  8.1 0.0 copy-start.4
  8.1 2.0 %collective-permute-start.8 = (bf16[800,384]{1,0:T(8,128)(2,1)S(1)}, bf16[800,384]{1,0:T(8,128)(2,1)S(1)}, u32[]{:S(2)}, u32[]{:S(2)}) collective-permute-start(bf16[800,384]{1,0:T(8,128)(2,1)S(1)} %get-tuple-element.53), channel_id=1, source_target_pairs={{0,4},{1,5},{2,6},{3,7},{4,0},{5,1},{6,2},{7,3},{8,12},{9,13},{10,... | collective-permute-start | bytes 1843208 | tf_op jit(solution)/shard_map/ppermute | solution.py:452
  10.2 0.9 %pack.4 = (bf16[816,384]{1,0:T(8,128)(2,1)S(1)}, bf16[816,384]{1,0:T(8,128)(2,1)S(1)}, bf16[208,384]{1,0:T(8,128)(2,1)S(1)}) custom-call(s32[1]{0:T(128)} %bitcast.idx_ref, bf16[3,2,192,1536]{3,2,1,0:T(8,128)(2,1)S(1)} %copy-done), custom_call_target="tpu_custom_call" | custom-call | tf_op jit(solution)/shard_map/pack/pallas_call | solution.py:162
  11.7 1.6 %collective-permute-start.7 = (bf16[800,384]{1,0:T(8,128)(2,1)S(1)}, bf16[800,384]{1,0:T(8,128)(2,1)S(1)}, u32[]{:S(2)}, u32[]{:S(2)}) collective-permute-start(bf16[800,384]{1,0:T(8,128)(2,1)S(1)} %get-tuple-element.47.refs_5_), channel_id=1, source_target_pairs={{0,2},{1,3},{2,0},{3,1},{4,6},{5,7},{6,4},{7,5},{8,10},{9,11},{10,... | collective-permute-start | bytes 1843208 | tf_op jit(solution)/shard_map/ppermute | solution.py:452
  13.3 1.6 %prep.1 = (f32[2,1536]{1,0:T(2,128)S(1)}, f32[2,1536,128]{2,1,0:T(8,128)S(1)}, bf16[384,1536]{1,0:T(8,128)(2,1)S(1)}, f8e5m2[384,1536]{1,0:T(32,128)(4,1)S(1)}, bf16[384,1536]{1,0:T(8,128)(2,1)S(1)}) custom-call(s32[1]{0:T(128)} %bitcast.idx_ref, s32[1]{0:T(128)S(6)} %copy.29.index_ref, f32[16]{0:T(128)S(1)} %copy-done.3, f32[3]{0:T(128)S(1)} %copy-done.4, ...), custom_call_target="tpu_custom_call" | custom-call | tf_op jit(solution)/shard_map/prep/pallas_call | solution.py:240
  14.9 13.7 %collective-permute-done.3.refs_2_ = bf16[416,384]{1,0:T(8,128)(2,1)S(1)} collective-permute-done((bf16[416,384]{1,0:T(8,128)(2,1)S(1)}, bf16[416,384]{1,0:T(8,128)(2,1)S(1)}, u32[]{:S(2)}, u32[]{:S(2)}) %collective-permute-start.3) | collective-permute-done | bytes 319520 | tf_op jit(solution)/shard_map/ppermute | solution.py:452
  28.6 0.5 collective-permute-done.2.refs_1_
  29.1 0.5 collective-permute-start.5
  29.7 2.8 %collective-permute-done.6.refs_7_ = bf16[416,384]{1,0:T(8,128)(2,1)S(1)} collective-permute-done((bf16[416,384]{1,0:T(8,128)(2,1)S(1)}, bf16[416,384]{1,0:T(8,128)(2,1)S(1)}, u32[]{:S(2)}, u32[]{:S(2)}) %collective-permute-start.6) | collective-permute-done | bytes 319520 | tf_op jit(solution)/shard_map/ppermute | solution.py:452
  32.5 8.4 %first.1 = (bf16[2,1536,1536]{2,1,0:T(8,128)(2,1)S(1)}, f32[384,1536]{1,0:T(8,128)S(1)}, bf16[384,1536]{1,0:T(8,128)(2,1)S(1)}, f8e5m2[384,1536]{1,0:T(32,128)(4,1)S(1)}) custom-call(s32[1]{0:T(128)} %bitcast.idx_ref, f32[2,1536]{1,0:T(2,128)S(1)} %get-tuple-element.40.refs_3_.hop_ref, f32[2,1536,128]{2,1,0:T(8,128)S(1)} %get-tuple-element.38.down_ref, ...), custom_call_target="tpu_custom_call" | custom-call | tf_op jit(solution)/shard_map/first/pallas_call | solution.py:481
  40.9 1.1 %collective-permute-start.11 = (bf16[816,384]{1,0:T(8,128)(2,1)S(1)}, bf16[816,384]{1,0:T(8,128)(2,1)S(1)}, u32[]{:S(2)}, u32[]{:S(2)}) collective-permute-start(bf16[816,384]{1,0:T(8,128)(2,1)S(1)} %get-tuple-element.65), channel_id=1, source_target_pairs={{0,2},{1,3},{2,0},{3,1},{4,6},{5,7},{6,4},{7,5},{8,10},{9,11},{10,... | collective-permute-start | bytes 1880072 | tf_op jit(solution)/shard_map/ppermute | solution.py:452
  42.0 1.0 %collective-permute-start.12 = (bf16[816,384]{1,0:T(8,128)(2,1)S(1)}, bf16[816,384]{1,0:T(8,128)(2,1)S(1)}, u32[]{:S(2)}, u32[]{:S(2)}) collective-permute-start(bf16[816,384]{1,0:T(8,128)(2,1)S(1)} %get-tuple-element.66), channel_id=1, source_target_pairs={{0,4},{1,5},{2,6},{3,7},{4,0},{5,1},{6,2},{7,3},{8,12},{9,13},{10,... | collective-permute-start | bytes 1880072 | tf_op jit(solution)/shard_map/ppermute | solution.py:452
  43.0 0.5 collective-permute-start.10
  43.5 1.4 %collective-permute-start.13 = (bf16[208,384]{1,0:T(8,128)(2,1)S(1)}, bf16[208,384]{1,0:T(8,128)(2,1)S(1)}, u32[]{:S(2)}, u32[]{:S(2)}) collective-permute-start(bf16[208,384]{1,0:T(8,128)(2,1)S(1)} %get-tuple-element.67), channel_id=1, source_target_pairs={{0,6},{1,7},{2,4},{3,5},{4,2},{5,3},{6,0},{7,1},{8,14},{9,15},{10,... | collective-permute-start | bytes 479240 | tf_op jit(solution)/shard_map/ppermute | solution.py:452
  44.9 0.1 collective-permute-done.9.refs_3_
  45.0 0.9 %collective-permute-done.10.refs_5_ = bf16[800,384]{1,0:T(8,128)(2,1)S(1)} collective-permute-done((bf16[800,384]{1,0:T(8,128)(2,1)S(1)}, bf16[800,384]{1,0:T(8,128)(2,1)S(1)}, u32[]{:S(2)}, u32[]{:S(2)}) %collective-permute-start.10) | collective-permute-done | bytes 614432 | tf_op jit(solution)/shard_map/ppermute | solution.py:452
  45.9 11.3 %second.1 = (bf16[384,1536]{1,0:T(8,128)(2,1)S(1)}, bf16[384,1536]{1,0:T(8,128)(2,1)S(1)}, f8e5m2[384,1536]{1,0:T(32,128)(4,1)S(1)}) custom-call(s32[1]{0:T(128)} %bitcast.idx_ref, bf16[384,1536]{1,0:T(8,128)(2,1)S(1)} %get-tuple-element.39.s1_ref, bf16[384,1536]{1,0:T(8,128)(2,1)S(1)} %get-tuple-element.51.refs_2_.w_hi.refs_3_, ...), custom_call_target="tpu_custom_call" | custom-call | tf_op jit(solution)/shard_map/second/pallas_call | solution.py:481
  57.2 6.2 %third.1 = (bf16[384,1536]{1,0:T(8,128)(2,1)S(1)}, f8e5m2[384,1536]{1,0:T(32,128)(4,1)S(1)}) custom-call(bf16[384,1536]{1,0:T(8,128)(2,1)S(1)} %get-tuple-element.56.hi, f8e5m2[384,1536]{1,0:T(32,128)(4,1)S(1)} %get-tuple-element.57.lo, bf16[2,1536,1536]{2,1,0:T(8,128)(2,1)S(1)} %get-tuple-element.58.scaled, f32[384,1536]{1,0:T(8,128)S(1)} %get-tuple-element.59.x), custom_call_target="tpu_custom_call" | custom-call | tf_op jit(solution)/shard_map/third/pallas_call | solution.py:481
  63.5 0.2 collective-permute-start.14
  63.7 0.4 collective-permute-start.15
  64.1 0.1 collective-permute-start.16
  64.2 4.5 %green_1.1.g1 = f32[2,192,1536]{2,1,0:T(8,128)S(1)} custom-call(s32[1]{0:T(128)} %bitcast.idx_ref, bf16[384,1536]{1,0:T(8,128)(2,1)S(1)} %get-tuple-element.62.left, bf16[2,1536,1536]{2,1,0:T(8,128)(2,1)S(1)} %get-tuple-element.58.scaled, bf16[3,2,192,1536]{3,2,1,0:T(8,128)(2,1)S(1)} %copy-done.1), custom_call_target="tpu_custom_call" | custom-call | tf_op jit(solution)/shard_map/green_1/pallas_call | solution.py:481
  68.8 8.7 %green_0.1 = f32[2,2,192,1536]{3,2,1,0:T(8,128)} custom-call(s32[1]{0:T(128)} %bitcast.idx_ref, f32[2,1536,128]{2,1,0:T(8,128)S(1)} %get-tuple-element.38.down_ref, bf16[384,1536]{1,0:T(8,128)(2,1)S(1)} %get-tuple-element.60.refs_3_.hi, f8e5m2[384,1536]{1,0:T(32,128)(4,1)S(1)} %get-tuple-element.61.lo, f32[2,192,1536]{2,1,0:T(8,128)S(1)} %green_1.1.g1, ...), custom_call_target="tpu_custom_call" | custom-call | tf_op jit(solution)/shard_map/green_0/pallas_call | solution.py:481
  (27 shorter events, 0.1 us)
Async XLA Ops:
  0.0 11.7 %collective-permute-start = (bf16[3,2,192,1536]{3,2,1,0:T(8,128)(2,1)}, bf16[3,2,192,1536]{3,2,1,0:T(8,128)(2,1)S(1)}, u32[]{:S(2)}, u32[]{:S(2)}) collective-permute-start(bf16[3,2,192,1536]{3,2,1,0:T(8,128)(2,1)} %refs_0_.5), channel_id=1, source_target_pairs={{0,1},{1,0},{2,3},{3,2},{4,5},{5,4},{6,7},{7,6},{8,9},{9,8},{10,11... | collective-permute-start | bytes 10616840 | tf_op jit(solution)/shard_map/ppermute | solution.py:452
  0.5 2.0 %copy-start = (bf16[3,2,192,1536]{3,2,1,0:T(8,128)(2,1)S(1)}, bf16[3,2,192,1536]{3,2,1,0:T(8,128)(2,1)}, u32[]{:S(2)}) copy-start(bf16[3,2,192,1536]{3,2,1,0:T(8,128)(2,1)} %refs_0_.5) | copy-start | bytes 10616836
  3.3 25.3 %collective-permute-start.1 = (bf16[784,384]{1,0:T(8,128)(2,1)S(1)}, bf16[784,384]{1,0:T(8,128)(2,1)S(1)}, u32[]{:S(2)}, u32[]{:S(2)}) collective-permute-start(bf16[784,384]{1,0:T(8,128)(2,1)S(1)} %get-tuple-element.43), channel_id=1, source_target_pairs={{0,2},{1,3},{2,0},{3,1},{4,6},{5,7},{6,4},{7,5},{8,10},{9,11},{10,... | collective-permute-start | bytes 1806344 | tf_op jit(solution)/shard_map/ppermute | solution.py:452
  5.9 23.3 %collective-permute-start.2 = (bf16[784,384]{1,0:T(8,128)(2,1)S(1)}, bf16[784,384]{1,0:T(8,128)(2,1)S(1)}, u32[]{:S(2)}, u32[]{:S(2)}) collective-permute-start(bf16[784,384]{1,0:T(8,128)(2,1)S(1)} %get-tuple-element.44), channel_id=1, source_target_pairs={{0,4},{1,5},{2,6},{3,7},{4,0},{5,1},{6,2},{7,3},{8,12},{9,13},{10,... | collective-permute-start | bytes 1806344 | tf_op jit(solution)/shard_map/ppermute | solution.py:452
  7.4 21.2 %collective-permute-start.3 = (bf16[416,384]{1,0:T(8,128)(2,1)S(1)}, bf16[416,384]{1,0:T(8,128)(2,1)S(1)}, u32[]{:S(2)}, u32[]{:S(2)}) collective-permute-start(bf16[416,384]{1,0:T(8,128)(2,1)S(1)} %get-tuple-element.45), channel_id=1, source_target_pairs={{0,6},{1,7},{2,4},{3,5},{4,2},{5,3},{6,0},{7,1},{8,14},{9,15},{10,... | collective-permute-start | bytes 958472 | tf_op jit(solution)/shard_map/ppermute | solution.py:452
  7.4 5.8 %copy-start.2 = (s32[3,1536]{1,0:T(4,128)S(1)}, s32[3,1536]{1,0:T(4,128)}, u32[]{:S(2)}) copy-start(s32[3,1536]{1,0:T(4,128)} %regions_ref.1) | copy-start | bytes 55300
  8.1 5.2 %copy-start.1 = (bf16[3,2,192,1536]{3,2,1,0:T(8,128)(2,1)S(1)}, bf16[3,2,192,1536]{3,2,1,0:T(8,128)(2,1)}, u32[]{:S(2)}) copy-start(bf16[3,2,192,1536]{3,2,1,0:T(8,128)(2,1)} %refs_0_.5) | copy-start | bytes 10616836
  8.1 5.2 %copy-start.3 = (f32[16]{0:T(128)S(1)}, f32[16]{0:T(128)}, u32[]{:S(2)}) copy-start(f32[16]{0:T(128)} %grid_ref.1) | copy-start | bytes 196
  8.1 5.2 %copy-start.4 = (f32[3]{0:T(128)S(1)}, f32[3]{0:T(128)}, u32[]{:S(2)}) copy-start(f32[3]{0:T(128)} %mass_ref.1) | copy-start | bytes 40
  8.1 5.2 %copy-start.5 = (f32[3]{0:T(128)S(1)}, f32[3]{0:T(128)}, u32[]{:S(2)}) copy-start(f32[3]{0:T(128)} %alpha_ref.1) | copy-start | bytes 40
  8.1 34.9 %collective-permute-start.8 = (bf16[800,384]{1,0:T(8,128)(2,1)S(1)}, bf16[800,384]{1,0:T(8,128)(2,1)S(1)}, u32[]{:S(2)}, u32[]{:S(2)}) collective-permute-start(bf16[800,384]{1,0:T(8,128)(2,1)S(1)} %get-tuple-element.53), channel_id=1, source_target_pairs={{0,4},{1,5},{2,6},{3,7},{4,0},{5,1},{6,2},{7,3},{8,12},{9,13},{10,... | collective-permute-start | bytes 1843208 | tf_op jit(solution)/shard_map/ppermute | solution.py:452
  11.7 31.3 %collective-permute-start.7 = (bf16[800,384]{1,0:T(8,128)(2,1)S(1)}, bf16[800,384]{1,0:T(8,128)(2,1)S(1)}, u32[]{:S(2)}, u32[]{:S(2)}) collective-permute-start(bf16[800,384]{1,0:T(8,128)(2,1)S(1)} %get-tuple-element.47.refs_5_), channel_id=1, source_target_pairs={{0,2},{1,3},{2,0},{3,1},{4,6},{5,7},{6,4},{7,5},{8,10},{9,11},{10,... | collective-permute-start | bytes 1843208 | tf_op jit(solution)/shard_map/ppermute | solution.py:452
  29.1 3.3 %collective-permute-start.4 = (bf16[784,384]{1,0:T(8,128)(2,1)S(1)}, bf16[784,384]{1,0:T(8,128)(2,1)S(1)}, u32[]{:S(2)}, u32[]{:S(2)}) collective-permute-start(bf16[784,384]{1,0:T(8,128)(2,1)S(1)} %get-tuple-element.48.refs_2_), channel_id=1, source_target_pairs={{0,1},{1,0},{2,3},{3,2},{4,5},{5,4},{6,7},{7,6},{8,9},{9,8},{10,11... | collective-permute-start | bytes 1806344 | tf_op jit(solution)/shard_map/ppermute | solution.py:452
  29.1 3.3 %collective-permute-start.5 = (bf16[784,384]{1,0:T(8,128)(2,1)S(1)}, bf16[784,384]{1,0:T(8,128)(2,1)S(1)}, u32[]{:S(2)}, u32[]{:S(2)}) collective-permute-start(bf16[784,384]{1,0:T(8,128)(2,1)S(1)} %get-tuple-element.49.refs_4_), channel_id=1, source_target_pairs={{0,1},{1,0},{2,3},{3,2},{4,5},{5,4},{6,7},{7,6},{8,9},{9,8},{10,11... | collective-permute-start | bytes 1806344 | tf_op jit(solution)/shard_map/ppermute | solution.py:452
  29.7 2.8 %collective-permute-start.6 = (bf16[416,384]{1,0:T(8,128)(2,1)S(1)}, bf16[416,384]{1,0:T(8,128)(2,1)S(1)}, u32[]{:S(2)}, u32[]{:S(2)}) collective-permute-start(bf16[416,384]{1,0:T(8,128)(2,1)S(1)} %get-tuple-element.50.refs_6_), channel_id=1, source_target_pairs={{0,1},{1,0},{2,3},{3,2},{4,5},{5,4},{6,7},{7,6},{8,9},{9,8},{10,11... | collective-permute-start | bytes 958472 | tf_op jit(solution)/shard_map/ppermute | solution.py:452
  40.9 22.6 %collective-permute-start.11 = (bf16[816,384]{1,0:T(8,128)(2,1)S(1)}, bf16[816,384]{1,0:T(8,128)(2,1)S(1)}, u32[]{:S(2)}, u32[]{:S(2)}) collective-permute-start(bf16[816,384]{1,0:T(8,128)(2,1)S(1)} %get-tuple-element.65), channel_id=1, source_target_pairs={{0,2},{1,3},{2,0},{3,1},{4,6},{5,7},{6,4},{7,5},{8,10},{9,11},{10,... | collective-permute-start | bytes 1880072 | tf_op jit(solution)/shard_map/ppermute | solution.py:452
  42.0 21.5 %collective-permute-start.12 = (bf16[816,384]{1,0:T(8,128)(2,1)S(1)}, bf16[816,384]{1,0:T(8,128)(2,1)S(1)}, u32[]{:S(2)}, u32[]{:S(2)}) collective-permute-start(bf16[816,384]{1,0:T(8,128)(2,1)S(1)} %get-tuple-element.66), channel_id=1, source_target_pairs={{0,4},{1,5},{2,6},{3,7},{4,0},{5,1},{6,2},{7,3},{8,12},{9,13},{10,... | collective-permute-start | bytes 1880072 | tf_op jit(solution)/shard_map/ppermute | solution.py:452
  43.0 2.0 %collective-permute-start.9 = (bf16[800,384]{1,0:T(8,128)(2,1)S(1)}, bf16[800,384]{1,0:T(8,128)(2,1)S(1)}, u32[]{:S(2)}, u32[]{:S(2)}) collective-permute-start(bf16[800,384]{1,0:T(8,128)(2,1)S(1)} %get-tuple-element.54.refs_2_), channel_id=1, source_target_pairs={{0,1},{1,0},{2,3},{3,2},{4,5},{5,4},{6,7},{7,6},{8,9},{9,8},{10,11... | collective-permute-start | bytes 1843208 | tf_op jit(solution)/shard_map/ppermute | solution.py:452
  43.0 2.9 %collective-permute-start.10 = (bf16[800,384]{1,0:T(8,128)(2,1)S(1)}, bf16[800,384]{1,0:T(8,128)(2,1)S(1)}, u32[]{:S(2)}, u32[]{:S(2)}) collective-permute-start(bf16[800,384]{1,0:T(8,128)(2,1)S(1)} %get-tuple-element.55.refs_4_), channel_id=1, source_target_pairs={{0,1},{1,0},{2,3},{3,2},{4,5},{5,4},{6,7},{7,6},{8,9},{9,8},{10,11... | collective-permute-start | bytes 1843208 | tf_op jit(solution)/shard_map/ppermute | solution.py:452
  43.5 20.0 %collective-permute-start.13 = (bf16[208,384]{1,0:T(8,128)(2,1)S(1)}, bf16[208,384]{1,0:T(8,128)(2,1)S(1)}, u32[]{:S(2)}, u32[]{:S(2)}) collective-permute-start(bf16[208,384]{1,0:T(8,128)(2,1)S(1)} %get-tuple-element.67), channel_id=1, source_target_pairs={{0,6},{1,7},{2,4},{3,5},{4,2},{5,3},{6,0},{7,1},{8,14},{9,15},{10,... | collective-permute-start | bytes 479240 | tf_op jit(solution)/shard_map/ppermute | solution.py:452
  63.5 5.2 %collective-permute-start.14 = (bf16[816,384]{1,0:T(8,128)(2,1)S(1)}, bf16[816,384]{1,0:T(8,128)(2,1)S(1)}, u32[]{:S(2)}, u32[]{:S(2)}) collective-permute-start(bf16[816,384]{1,0:T(8,128)(2,1)S(1)} %get-tuple-element.68.refs_2_), channel_id=1, source_target_pairs={{0,1},{1,0},{2,3},{3,2},{4,5},{5,4},{6,7},{7,6},{8,9},{9,8},{10,11... | collective-permute-start | bytes 1880072 | tf_op jit(solution)/shard_map/ppermute | solution.py:452
  63.7 5.0 %collective-permute-start.15 = (bf16[816,384]{1,0:T(8,128)(2,1)S(1)}, bf16[816,384]{1,0:T(8,128)(2,1)S(1)}, u32[]{:S(2)}, u32[]{:S(2)}) collective-permute-start(bf16[816,384]{1,0:T(8,128)(2,1)S(1)} %get-tuple-element.69.refs_4_), channel_id=1, source_target_pairs={{0,1},{1,0},{2,3},{3,2},{4,5},{5,4},{6,7},{7,6},{8,9},{9,8},{10,11... | collective-permute-start | bytes 1880072 | tf_op jit(solution)/shard_map/ppermute | solution.py:452
  64.1 4.6 %collective-permute-start.16 = (bf16[208,384]{1,0:T(8,128)(2,1)S(1)}, bf16[208,384]{1,0:T(8,128)(2,1)S(1)}, u32[]{:S(2)}, u32[]{:S(2)}) collective-permute-start(bf16[208,384]{1,0:T(8,128)(2,1)S(1)} %get-tuple-element.70.refs_6_), channel_id=1, source_target_pairs={{0,1},{1,0},{2,3},{3,2},{4,5},{5,4},{6,7},{7,6},{8,9},{9,8},{10,11... | collective-permute-start | bytes 479240 | tf_op jit(solution)/shard_map/ppermute | solution.py:452

commit v4 on v3

--- a/solution.py
+++ b/solution.py
@@ -296,8 +296,9 @@
     col = lax.broadcasted_iota(jnp.int32, (m, m), 1)
     for which in (1, 2, 3):
         here = slice(which * m, (which + 1) * m)
-        packed = whole[0, here, here].astype(F32)
-        flipped = packed.T
+        packed = whole[0, here, here]
+        flipped = packed.T.astype(F32)
+        packed = packed.astype(F32)
         diag = diags[which - 1, 0].astype(F32) + diags[which - 1, 1].astype(F32)
         diag = jnp.broadcast_to(diag[0:1, :], (m, m))
         real = jnp.where(col >= row, packed, flipped)
@@ -362,7 +363,9 @@
 
 
 def scale_rows(plane, down_ref, index):
-    return (plane.astype(F32) * down_ref[index, :, 0:1]).astype(BF16)
+    down = down_ref[index]
+    down = jnp.concatenate([down] * (plane.shape[1] // down.shape[1]), axis=1)
+    return (plane.astype(F32) * down).astype(BF16)
 
 
 def second_kernel(s, idx_ref, s1_ref, w_hi, w_lo, *refs):

time: 77.8 us -> 77.1 us (level)
  no operation moved by 1% of the time
where the time goes in v4:
time: 77.1 us; the launch traced here: 76.9 us
  Pallas kernels  42.4 us (55%)
  waiting for transfers between devices  18.1 us (23%)
  starting transfers between devices  13.4 us (17%)
  local copies, waits for them, and re-layouts  2.03 us (3%)
  between operations  1.02 us (1%)
    pallas_call x5, Pallas kernels, call(): pl.pallas_call(functools.partial(kernel, s), in_specs=[SMEM if x is idx e...  38.4 us
    ppermute x17, waiting for transfers between devices, swap(): return lax.ppermute(x, 'cols', [(i, i ^ mask) for i in range(n)])  18.1 us
    ppermute x17, starting transfers between devices, swap(): return lax.ppermute(x, 'cols', [(i, i ^ mask) for i in range(n)])  13.4 us
    pallas_call x3, Pallas kernels, pack(): pl.pallas_call(functools.partial(pack_kernel, s, index, heads), in_specs=...  2.37 us
    unnamed x12, local copies, waits for them, and re-layouts  2.03 us
    pallas_call x1, Pallas kernels, prep(): pl.pallas_call(functools.partial(prep_kernel, s), grid=(1,), in_specs=[SM...  1.61 us
  transfers between devices with their start and end apart: 17, of which 5 were waited for; matrix products, arithmetic and copies ran while one was open for 0% of the time, Pallas kernels for 44%

profile of v4, /device:TPU:0, one launch (start us, length us, event | category | flops | bytes accessed | tf_op | source)
XLA Modules:
  0.0 76.9 jit_solution(5396410681450033234)
XLA Ops:
  0.0 0.5 collective-permute-start
  0.5 2.0 %copy-done = bf16[3,2,192,1536]{3,2,1,0:T(8,128)(2,1)S(1)} copy-done((bf16[3,2,192,1536]{3,2,1,0:T(8,128)(2,1)S(1)}, bf16[3,2,192,1536]{3,2,1,0:T(8,128)(2,1)}, u32[]{:S(2)}) %copy-start) | copy-done | bytes 3538968
  2.5 0.8 %pack.3 = (bf16[784,384]{1,0:T(8,128)(2,1)S(1)}, bf16[784,384]{1,0:T(8,128)(2,1)S(1)}, bf16[416,384]{1,0:T(8,128)(2,1)S(1)}) custom-call(s32[1]{0:T(128)} %bitcast.idx_ref, bf16[3,2,192,1536]{3,2,1,0:T(8,128)(2,1)S(1)} %copy-done), custom_call_target="tpu_custom_call" | custom-call | tf_op jit(solution)/shard_map/pack/pallas_call | solution.py:162
  3.3 2.6 %collective-permute-start.1 = (bf16[784,384]{1,0:T(8,128)(2,1)S(1)}, bf16[784,384]{1,0:T(8,128)(2,1)S(1)}, u32[]{:S(2)}, u32[]{:S(2)}) collective-permute-start(bf16[784,384]{1,0:T(8,128)(2,1)S(1)} %get-tuple-element.43), channel_id=1, source_target_pairs={{0,2},{1,3},{2,0},{3,1},{4,6},{5,7},{6,4},{7,5},{8,10},{9,11},{10,... | collective-permute-start | bytes 1806344 | tf_op jit(solution)/shard_map/ppermute | solution.py:455
  5.9 1.5 %collective-permute-start.2 = (bf16[784,384]{1,0:T(8,128)(2,1)S(1)}, bf16[784,384]{1,0:T(8,128)(2,1)S(1)}, u32[]{:S(2)}, u32[]{:S(2)}) collective-permute-start(bf16[784,384]{1,0:T(8,128)(2,1)S(1)} %get-tuple-element.44), channel_id=1, source_target_pairs={{0,4},{1,5},{2,6},{3,7},{4,0},{5,1},{6,2},{7,3},{8,12},{9,13},{10,... | collective-permute-start | bytes 1806344 | tf_op jit(solution)/shard_map/ppermute | solution.py:455
  7.4 0.0 collective-permute-start.3
  7.4 0.6 pack.5
  8.1 0.0 copy-start.1
  8.1 0.0 copy-start.3
  8.1 0.0 copy-start.4
  8.1 2.0 %collective-permute-start.8 = (bf16[800,384]{1,0:T(8,128)(2,1)S(1)}, bf16[800,384]{1,0:T(8,128)(2,1)S(1)}, u32[]{:S(2)}, u32[]{:S(2)}) collective-permute-start(bf16[800,384]{1,0:T(8,128)(2,1)S(1)} %get-tuple-element.53), channel_id=1, source_target_pairs={{0,4},{1,5},{2,6},{3,7},{4,0},{5,1},{6,2},{7,3},{8,12},{9,13},{10,... | collective-permute-start | bytes 1843208 | tf_op jit(solution)/shard_map/ppermute | solution.py:455
  10.2 0.9 %pack.4 = (bf16[816,384]{1,0:T(8,128)(2,1)S(1)}, bf16[816,384]{1,0:T(8,128)(2,1)S(1)}, bf16[208,384]{1,0:T(8,128)(2,1)S(1)}) custom-call(s32[1]{0:T(128)} %bitcast.idx_ref, bf16[3,2,192,1536]{3,2,1,0:T(8,128)(2,1)S(1)} %copy-done), custom_call_target="tpu_custom_call" | custom-call | tf_op jit(solution)/shard_map/pack/pallas_call | solution.py:162
  11.7 1.6 %collective-permute-start.7 = (bf16[800,384]{1,0:T(8,128)(2,1)S(1)}, bf16[800,384]{1,0:T(8,128)(2,1)S(1)}, u32[]{:S(2)}, u32[]{:S(2)}) collective-permute-start(bf16[800,384]{1,0:T(8,128)(2,1)S(1)} %get-tuple-element.47.refs_5_), channel_id=1, source_target_pairs={{0,2},{1,3},{2,0},{3,1},{4,6},{5,7},{6,4},{7,5},{8,10},{9,11},{10,... | collective-permute-start | bytes 1843208 | tf_op jit(solution)/shard_map/ppermute | solution.py:455
  13.3 1.6 %prep.1 = (f32[2,1536]{1,0:T(2,128)S(1)}, f32[2,1536,128]{2,1,0:T(8,128)S(1)}, bf16[384,1536]{1,0:T(8,128)(2,1)S(1)}, f8e5m2[384,1536]{1,0:T(32,128)(4,1)S(1)}, bf16[384,1536]{1,0:T(8,128)(2,1)S(1)}) custom-call(s32[1]{0:T(128)} %bitcast.idx_ref, s32[1]{0:T(128)S(6)} %copy.29.index_ref, f32[16]{0:T(128)S(1)} %copy-done.3, f32[3]{0:T(128)S(1)} %copy-done.4, ...), custom_call_target="tpu_custom_call" | custom-call | tf_op jit(solution)/shard_map/prep/pallas_call | solution.py:240
  14.9 13.7 %collective-permute-done.3.refs_2_ = bf16[416,384]{1,0:T(8,128)(2,1)S(1)} collective-permute-done((bf16[416,384]{1,0:T(8,128)(2,1)S(1)}, bf16[416,384]{1,0:T(8,128)(2,1)S(1)}, u32[]{:S(2)}, u32[]{:S(2)}) %collective-permute-start.3) | collective-permute-done | bytes 319520 | tf_op jit(solution)/shard_map/ppermute | solution.py:455
  28.6 0.5 collective-permute-done.2.refs_1_
  29.1 0.5 collective-permute-start.5
  29.7 2.8 %collective-permute-done.6.refs_7_ = bf16[416,384]{1,0:T(8,128)(2,1)S(1)} collective-permute-done((bf16[416,384]{1,0:T(8,128)(2,1)S(1)}, bf16[416,384]{1,0:T(8,128)(2,1)S(1)}, u32[]{:S(2)}, u32[]{:S(2)}) %collective-permute-start.6) | collective-permute-done | bytes 319520 | tf_op jit(solution)/shard_map/ppermute | solution.py:455
  32.5 7.9 %first.1 = (bf16[2,1536,1536]{2,1,0:T(8,128)(2,1)S(1)}, f32[384,1536]{1,0:T(8,128)S(1)}, bf16[384,1536]{1,0:T(8,128)(2,1)S(1)}, f8e5m2[384,1536]{1,0:T(32,128)(4,1)S(1)}) custom-call(s32[1]{0:T(128)} %bitcast.idx_ref, f32[2,1536]{1,0:T(2,128)S(1)} %get-tuple-element.40.refs_3_.hop_ref, f32[2,1536,128]{2,1,0:T(8,128)S(1)} %get-tuple-element.38.down_ref, ...), custom_call_target="tpu_custom_call" | custom-call | tf_op jit(solution)/shard_map/first/pallas_call | solution.py:484
  40.4 1.1 %collective-permute-start.11 = (bf16[816,384]{1,0:T(8,128)(2,1)S(1)}, bf16[816,384]{1,0:T(8,128)(2,1)S(1)}, u32[]{:S(2)}, u32[]{:S(2)}) collective-permute-start(bf16[816,384]{1,0:T(8,128)(2,1)S(1)} %get-tuple-element.65), channel_id=1, source_target_pairs={{0,2},{1,3},{2,0},{3,1},{4,6},{5,7},{6,4},{7,5},{8,10},{9,11},{10,... | collective-permute-start | bytes 1880072 | tf_op jit(solution)/shard_map/ppermute | solution.py:455
  41.5 1.0 %collective-permute-start.12 = (bf16[816,384]{1,0:T(8,128)(2,1)S(1)}, bf16[816,384]{1,0:T(8,128)(2,1)S(1)}, u32[]{:S(2)}, u32[]{:S(2)}) collective-permute-start(bf16[816,384]{1,0:T(8,128)(2,1)S(1)} %get-tuple-element.66), channel_id=1, source_target_pairs={{0,4},{1,5},{2,6},{3,7},{4,0},{5,1},{6,2},{7,3},{8,12},{9,13},{10,... | collective-permute-start | bytes 1880072 | tf_op jit(solution)/shard_map/ppermute | solution.py:455
  42.5 0.5 collective-permute-start.10
  43.0 1.4 %collective-permute-start.13 = (bf16[208,384]{1,0:T(8,128)(2,1)S(1)}, bf16[208,384]{1,0:T(8,128)(2,1)S(1)}, u32[]{:S(2)}, u32[]{:S(2)}) collective-permute-start(bf16[208,384]{1,0:T(8,128)(2,1)S(1)} %get-tuple-element.67), channel_id=1, source_target_pairs={{0,6},{1,7},{2,4},{3,5},{4,2},{5,3},{6,0},{7,1},{8,14},{9,15},{10,... | collective-permute-start | bytes 479240 | tf_op jit(solution)/shard_map/ppermute | solution.py:455
  44.4 0.1 collective-permute-done.9.refs_3_
  44.5 0.9 %collective-permute-done.10.refs_5_ = bf16[800,384]{1,0:T(8,128)(2,1)S(1)} collective-permute-done((bf16[800,384]{1,0:T(8,128)(2,1)S(1)}, bf16[800,384]{1,0:T(8,128)(2,1)S(1)}, u32[]{:S(2)}, u32[]{:S(2)}) %collective-permute-start.10) | collective-permute-done | bytes 614432 | tf_op jit(solution)/shard_map/ppermute | solution.py:455
  45.4 11.4 %second.1 = (bf16[384,1536]{1,0:T(8,128)(2,1)S(1)}, bf16[384,1536]{1,0:T(8,128)(2,1)S(1)}, f8e5m2[384,1536]{1,0:T(32,128)(4,1)S(1)}) custom-call(s32[1]{0:T(128)} %bitcast.idx_ref, bf16[384,1536]{1,0:T(8,128)(2,1)S(1)} %get-tuple-element.39.s1_ref, bf16[384,1536]{1,0:T(8,128)(2,1)S(1)} %get-tuple-element.51.refs_2_.w_hi.refs_3_, ...), custom_call_target="tpu_custom_call" | custom-call | tf_op jit(solution)/shard_map/second/pallas_call | solution.py:484
  56.8 6.2 %third.1 = (bf16[384,1536]{1,0:T(8,128)(2,1)S(1)}, f8e5m2[384,1536]{1,0:T(32,128)(4,1)S(1)}) custom-call(bf16[384,1536]{1,0:T(8,128)(2,1)S(1)} %get-tuple-element.56.hi, f8e5m2[384,1536]{1,0:T(32,128)(4,1)S(1)} %get-tuple-element.57.lo, bf16[2,1536,1536]{2,1,0:T(8,128)(2,1)S(1)} %get-tuple-element.58.scaled, f32[384,1536]{1,0:T(8,128)S(1)} %get-tuple-element.59.x), custom_call_target="tpu_custom_call" | custom-call | tf_op jit(solution)/shard_map/third/pallas_call | solution.py:484
  63.1 0.2 collective-permute-start.14
  63.3 0.4 collective-permute-start.15
  63.6 0.1 collective-permute-start.16
  63.8 4.5 %green_1.1.g1 = f32[2,192,1536]{2,1,0:T(8,128)S(1)} custom-call(s32[1]{0:T(128)} %bitcast.idx_ref, bf16[384,1536]{1,0:T(8,128)(2,1)S(1)} %get-tuple-element.62.left, bf16[2,1536,1536]{2,1,0:T(8,128)(2,1)S(1)} %get-tuple-element.58.scaled, bf16[3,2,192,1536]{3,2,1,0:T(8,128)(2,1)S(1)} %copy-done.1), custom_call_target="tpu_custom_call" | custom-call | tf_op jit(solution)/shard_map/green_1/pallas_call | solution.py:484
  68.3 8.5 %green_0.1 = f32[2,2,192,1536]{3,2,1,0:T(8,128)} custom-call(s32[1]{0:T(128)} %bitcast.idx_ref, f32[2,1536,128]{2,1,0:T(8,128)S(1)} %get-tuple-element.38.down_ref, bf16[384,1536]{1,0:T(8,128)(2,1)S(1)} %get-tuple-element.60.refs_3_.hi, f8e5m2[384,1536]{1,0:T(32,128)(4,1)S(1)} %get-tuple-element.61.lo, f32[2,192,1536]{2,1,0:T(8,128)S(1)} %green_1.1.g1, ...), custom_call_target="tpu_custom_call" | custom-call | tf_op jit(solution)/shard_map/green_0/pallas_call | solution.py:484
  (27 shorter events, 0.1 us)
Async XLA Ops:
  0.0 11.7 %collective-permute-start = (bf16[3,2,192,1536]{3,2,1,0:T(8,128)(2,1)}, bf16[3,2,192,1536]{3,2,1,0:T(8,128)(2,1)S(1)}, u32[]{:S(2)}, u32[]{:S(2)}) collective-permute-start(bf16[3,2,192,1536]{3,2,1,0:T(8,128)(2,1)} %refs_0_.5), channel_id=1, source_target_pairs={{0,1},{1,0},{2,3},{3,2},{4,5},{5,4},{6,7},{7,6},{8,9},{9,8},{10,11... | collective-permute-start | bytes 10616840 | tf_op jit(solution)/shard_map/ppermute | solution.py:455
  0.5 2.0 %copy-start = (bf16[3,2,192,1536]{3,2,1,0:T(8,128)(2,1)S(1)}, bf16[3,2,192,1536]{3,2,1,0:T(8,128)(2,1)}, u32[]{:S(2)}) copy-start(bf16[3,2,192,1536]{3,2,1,0:T(8,128)(2,1)} %refs_0_.5) | copy-start | bytes 10616836
  3.3 25.3 %collective-permute-start.1 = (bf16[784,384]{1,0:T(8,128)(2,1)S(1)}, bf16[784,384]{1,0:T(8,128)(2,1)S(1)}, u32[]{:S(2)}, u32[]{:S(2)}) collective-permute-start(bf16[784,384]{1,0:T(8,128)(2,1)S(1)} %get-tuple-element.43), channel_id=1, source_target_pairs={{0,2},{1,3},{2,0},{3,1},{4,6},{5,7},{6,4},{7,5},{8,10},{9,11},{10,... | collective-permute-start | bytes 1806344 | tf_op jit(solution)/shard_map/ppermute | solution.py:455
  5.9 23.3 %collective-permute-start.2 = (bf16[784,384]{1,0:T(8,128)(2,1)S(1)}, bf16[784,384]{1,0:T(8,128)(2,1)S(1)}, u32[]{:S(2)}, u32[]{:S(2)}) collective-permute-start(bf16[784,384]{1,0:T(8,128)(2,1)S(1)} %get-tuple-element.44), channel_id=1, source_target_pairs={{0,4},{1,5},{2,6},{3,7},{4,0},{5,1},{6,2},{7,3},{8,12},{9,13},{10,... | collective-permute-start | bytes 1806344 | tf_op jit(solution)/shard_map/ppermute | solution.py:455
  7.4 21.2 %collective-permute-start.3 = (bf16[416,384]{1,0:T(8,128)(2,1)S(1)}, bf16[416,384]{1,0:T(8,128)(2,1)S(1)}, u32[]{:S(2)}, u32[]{:S(2)}) collective-permute-start(bf16[416,384]{1,0:T(8,128)(2,1)S(1)} %get-tuple-element.45), channel_id=1, source_target_pairs={{0,6},{1,7},{2,4},{3,5},{4,2},{5,3},{6,0},{7,1},{8,14},{9,15},{10,... | collective-permute-start | bytes 958472 | tf_op jit(solution)/shard_map/ppermute | solution.py:455
  7.4 5.8 %copy-start.2 = (s32[3,1536]{1,0:T(4,128)S(1)}, s32[3,1536]{1,0:T(4,128)}, u32[]{:S(2)}) copy-start(s32[3,1536]{1,0:T(4,128)} %regions_ref.1) | copy-start | bytes 55300
  8.1 5.2 %copy-start.1 = (bf16[3,2,192,1536]{3,2,1,0:T(8,128)(2,1)S(1)}, bf16[3,2,192,1536]{3,2,1,0:T(8,128)(2,1)}, u32[]{:S(2)}) copy-start(bf16[3,2,192,1536]{3,2,1,0:T(8,128)(2,1)} %refs_0_.5) | copy-start | bytes 10616836
  8.1 5.2 %copy-start.3 = (f32[16]{0:T(128)S(1)}, f32[16]{0:T(128)}, u32[]{:S(2)}) copy-start(f32[16]{0:T(128)} %grid_ref.1) | copy-start | bytes 196
  8.1 5.2 %copy-start.4 = (f32[3]{0:T(128)S(1)}, f32[3]{0:T(128)}, u32[]{:S(2)}) copy-start(f32[3]{0:T(128)} %mass_ref.1) | copy-start | bytes 40
  8.1 5.2 %copy-start.5 = (f32[3]{0:T(128)S(1)}, f32[3]{0:T(128)}, u32[]{:S(2)}) copy-start(f32[3]{0:T(128)} %alpha_ref.1) | copy-start | bytes 40
  8.1 34.4 %collective-permute-start.8 = (bf16[800,384]{1,0:T(8,128)(2,1)S(1)}, bf16[800,384]{1,0:T(8,128)(2,1)S(1)}, u32[]{:S(2)}, u32[]{:S(2)}) collective-permute-start(bf16[800,384]{1,0:T(8,128)(2,1)S(1)} %get-tuple-element.53), channel_id=1, source_target_pairs={{0,4},{1,5},{2,6},{3,7},{4,0},{5,1},{6,2},{7,3},{8,12},{9,13},{10,... | collective-permute-start | bytes 1843208 | tf_op jit(solution)/shard_map/ppermute | solution.py:455
  11.7 30.8 %collective-permute-start.7 = (bf16[800,384]{1,0:T(8,128)(2,1)S(1)}, bf16[800,384]{1,0:T(8,128)(2,1)S(1)}, u32[]{:S(2)}, u32[]{:S(2)}) collective-permute-start(bf16[800,384]{1,0:T(8,128)(2,1)S(1)} %get-tuple-element.47.refs_5_), channel_id=1, source_target_pairs={{0,2},{1,3},{2,0},{3,1},{4,6},{5,7},{6,4},{7,5},{8,10},{9,11},{10,... | collective-permute-start | bytes 1843208 | tf_op jit(solution)/shard_map/ppermute | solution.py:455
  29.1 3.3 %collective-permute-start.4 = (bf16[784,384]{1,0:T(8,128)(2,1)S(1)}, bf16[784,384]{1,0:T(8,128)(2,1)S(1)}, u32[]{:S(2)}, u32[]{:S(2)}) collective-permute-start(bf16[784,384]{1,0:T(8,128)(2,1)S(1)} %get-tuple-element.48.refs_2_), channel_id=1, source_target_pairs={{0,1},{1,0},{2,3},{3,2},{4,5},{5,4},{6,7},{7,6},{8,9},{9,8},{10,11... | collective-permute-start | bytes 1806344 | tf_op jit(solution)/shard_map/ppermute | solution.py:455
  29.1 3.3 %collective-permute-start.5 = (bf16[784,384]{1,0:T(8,128)(2,1)S(1)}, bf16[784,384]{1,0:T(8,128)(2,1)S(1)}, u32[]{:S(2)}, u32[]{:S(2)}) collective-permute-start(bf16[784,384]{1,0:T(8,128)(2,1)S(1)} %get-tuple-element.49.refs_4_), channel_id=1, source_target_pairs={{0,1},{1,0},{2,3},{3,2},{4,5},{5,4},{6,7},{7,6},{8,9},{9,8},{10,11... | collective-permute-start | bytes 1806344 | tf_op jit(solution)/shard_map/ppermute | solution.py:455
  29.7 2.8 %collective-permute-start.6 = (bf16[416,384]{1,0:T(8,128)(2,1)S(1)}, bf16[416,384]{1,0:T(8,128)(2,1)S(1)}, u32[]{:S(2)}, u32[]{:S(2)}) collective-permute-start(bf16[416,384]{1,0:T(8,128)(2,1)S(1)} %get-tuple-element.50.refs_6_), channel_id=1, source_target_pairs={{0,1},{1,0},{2,3},{3,2},{4,5},{5,4},{6,7},{7,6},{8,9},{9,8},{10,11... | collective-permute-start | bytes 958472 | tf_op jit(solution)/shard_map/ppermute | solution.py:455
  40.4 22.7 %collective-permute-start.11 = (bf16[816,384]{1,0:T(8,128)(2,1)S(1)}, bf16[816,384]{1,0:T(8,128)(2,1)S(1)}, u32[]{:S(2)}, u32[]{:S(2)}) collective-permute-start(bf16[816,384]{1,0:T(8,128)(2,1)S(1)} %get-tuple-element.65), channel_id=1, source_target_pairs={{0,2},{1,3},{2,0},{3,1},{4,6},{5,7},{6,4},{7,5},{8,10},{9,11},{10,... | collective-permute-start | bytes 1880072 | tf_op jit(solution)/shard_map/ppermute | solution.py:455
  41.5 21.6 %collective-permute-start.12 = (bf16[816,384]{1,0:T(8,128)(2,1)S(1)}, bf16[816,384]{1,0:T(8,128)(2,1)S(1)}, u32[]{:S(2)}, u32[]{:S(2)}) collective-permute-start(bf16[816,384]{1,0:T(8,128)(2,1)S(1)} %get-tuple-element.66), channel_id=1, source_target_pairs={{0,4},{1,5},{2,6},{3,7},{4,0},{5,1},{6,2},{7,3},{8,12},{9,13},{10,... | collective-permute-start | bytes 1880072 | tf_op jit(solution)/shard_map/ppermute | solution.py:455
  42.5 2.0 %collective-permute-start.9 = (bf16[800,384]{1,0:T(8,128)(2,1)S(1)}, bf16[800,384]{1,0:T(8,128)(2,1)S(1)}, u32[]{:S(2)}, u32[]{:S(2)}) collective-permute-start(bf16[800,384]{1,0:T(8,128)(2,1)S(1)} %get-tuple-element.54.refs_2_), channel_id=1, source_target_pairs={{0,1},{1,0},{2,3},{3,2},{4,5},{5,4},{6,7},{7,6},{8,9},{9,8},{10,11... | collective-permute-start | bytes 1843208 | tf_op jit(solution)/shard_map/ppermute | solution.py:455
  42.5 2.9 %collective-permute-start.10 = (bf16[800,384]{1,0:T(8,128)(2,1)S(1)}, bf16[800,384]{1,0:T(8,128)(2,1)S(1)}, u32[]{:S(2)}, u32[]{:S(2)}) collective-permute-start(bf16[800,384]{1,0:T(8,128)(2,1)S(1)} %get-tuple-element.55.refs_4_), channel_id=1, source_target_pairs={{0,1},{1,0},{2,3},{3,2},{4,5},{5,4},{6,7},{7,6},{8,9},{9,8},{10,11... | collective-permute-start | bytes 1843208 | tf_op jit(solution)/shard_map/ppermute | solution.py:455
  43.0 20.0 %collective-permute-start.13 = (bf16[208,384]{1,0:T(8,128)(2,1)S(1)}, bf16[208,384]{1,0:T(8,128)(2,1)S(1)}, u32[]{:S(2)}, u32[]{:S(2)}) collective-permute-start(bf16[208,384]{1,0:T(8,128)(2,1)S(1)} %get-tuple-element.67), channel_id=1, source_target_pairs={{0,6},{1,7},{2,4},{3,5},{4,2},{5,3},{6,0},{7,1},{8,14},{9,15},{10,... | collective-permute-start | bytes 479240 | tf_op jit(solution)/shard_map/ppermute | solution.py:455
  63.1 5.2 %collective-permute-start.14 = (bf16[816,384]{1,0:T(8,128)(2,1)S(1)}, bf16[816,384]{1,0:T(8,128)(2,1)S(1)}, u32[]{:S(2)}, u32[]{:S(2)}) collective-permute-start(bf16[816,384]{1,0:T(8,128)(2,1)S(1)} %get-tuple-element.68.refs_2_), channel_id=1, source_target_pairs={{0,1},{1,0},{2,3},{3,2},{4,5},{5,4},{6,7},{7,6},{8,9},{9,8},{10,11... | collective-permute-start | bytes 1880072 | tf_op jit(solution)/shard_map/ppermute | solution.py:455
  63.3 5.0 %collective-permute-start.15 = (bf16[816,384]{1,0:T(8,128)(2,1)S(1)}, bf16[816,384]{1,0:T(8,128)(2,1)S(1)}, u32[]{:S(2)}, u32[]{:S(2)}) collective-permute-start(bf16[816,384]{1,0:T(8,128)(2,1)S(1)} %get-tuple-element.69.refs_4_), channel_id=1, source_target_pairs={{0,1},{1,0},{2,3},{3,2},{4,5},{5,4},{6,7},{7,6},{8,9},{9,8},{10,11... | collective-permute-start | bytes 1880072 | tf_op jit(solution)/shard_map/ppermute | solution.py:455
  63.6 4.6 %collective-permute-start.16 = (bf16[208,384]{1,0:T(8,128)(2,1)S(1)}, bf16[208,384]{1,0:T(8,128)(2,1)S(1)}, u32[]{:S(2)}, u32[]{:S(2)}) collective-permute-start(bf16[208,384]{1,0:T(8,128)(2,1)S(1)} %get-tuple-element.70.refs_6_), channel_id=1, source_target_pairs={{0,1},{1,0},{2,3},{3,2},{4,5},{5,4},{6,7},{7,6},{8,9},{9,8},{10,11... | collective-permute-start | bytes 479240 | tf_op jit(solution)/shard_map/ppermute | solution.py:455
